TPU v7x, 128 devices: a whole 4x4x4 slice. The times are simulated.
128 devices in a mesh: dp: 2 (over core), context: 8 (over z, x_hi), experts: 8 (over x_lo, y).
Axes of the slice: x: 4 (x_hi: 2, x_lo: 2; x = x_hi * 2 + x_lo), y: 4, z: 4, core: 2. Of those that a mesh axis runs over, the one named last changes fastest.
Arguments:
- tokens: bfloat16 [16, 1024, 1536], P(('dp', 'experts'), 'context'), may hold values from -6 to 6
- cotangent: bfloat16 [16, 1024, 1536], P(('dp', 'experts'), 'context'), may hold values from -6 to 6
- expert_ids: int32 [2, 16, 1024, 4], P(None, ('dp', 'experts'), 'context'), may hold values from 0 to 15, all different within a row; in each aligned block of 128 rows (0 to 127, 128 to 255, ..., all dimensions but the last counted through in order) at most 40 rows name the same one
- gate_values: float32 [2, 16, 1024, 4], P(None, ('dp', 'experts'), 'context'), may hold values from 0.1 to 0.4
- block_order: int32 [16, 8], P(('dp', 'experts')), may hold values from 0 to 7, each once within a row
- qkv_weight: float32 [2, 1536, 2048], P(None, ('dp', 'context', 'experts')), may hold values from -0.15625 to 0.15625
- qkv_first: float32 [2, 1536, 2048], P(None, ('dp', 'context', 'experts'))
- qkv_second: float32 [2, 1536, 2048], P(None, ('dp', 'context', 'experts')), as said below
- out_weight: float32 [2, 1536, 1536], P(None, None, ('dp', 'context', 'experts')), may hold values from -0.625 to 0.625
- out_first: float32 [2, 1536, 1536], P(None, None, ('dp', 'context', 'experts'))
- out_second: float32 [2, 1536, 1536], P(None, None, ('dp', 'context', 'experts')), as said below
- in_weight: float32 [2, 16, 1536, 1536], P(None, 'experts', ('dp', 'context')), may hold values from -0.15625 to 0.15625
- in_first: float32 [2, 16, 1536, 1536], P(None, 'experts', ('dp', 'context'))
- in_second: float32 [2, 16, 1536, 1536], P(None, 'experts', ('dp', 'context')), as said below
- down_weight: float32 [2, 16, 768, 1536], P(None, 'experts', None, ('dp', 'context')), may hold values from -0.4375 to 0.4375
- down_first: float32 [2, 16, 768, 1536], P(None, 'experts', None, ('dp', 'context'))
- down_second: float32 [2, 16, 768, 1536], P(None, 'experts', None, ('dp', 'context')), as said below
- norm_gains: float32 [2, 2, 1536], P(None, None, ('dp', 'context', 'experts')), may hold values from 0.5 to 1.5
- gain_first: float32 [2, 2, 1536], P(None, None, ('dp', 'context', 'experts'))
- gain_second: float32 [2, 2, 1536], P(None, None, ('dp', 'context', 'experts')), as said below
Outputs:
- result: bfloat16 [16, 1024, 1536], P(('dp', 'experts'), 'context')
- input_grad: float32 [16, 1024, 1536], P(('dp', 'experts'), 'context')
- qkv_new: float32 [2, 1536, 2048], P(None, ('dp', 'context', 'experts'))
- qkv_first_new: float32 [2, 1536, 2048], P(None, ('dp', 'context', 'experts'))
- qkv_second_new: float32 [2, 1536, 2048], P(None, ('dp', 'context', 'experts'))
- out_new: float32 [2, 1536, 1536], P(None, None, ('dp', 'context', 'experts'))
- out_first_new: float32 [2, 1536, 1536], P(None, None, ('dp', 'context', 'experts'))
- out_second_new: float32 [2, 1536, 1536], P(None, None, ('dp', 'context', 'experts'))
- in_new: float32 [2, 16, 1536, 1536], P(None, 'experts', ('dp', 'context'))
- in_first_new: float32 [2, 16, 1536, 1536], P(None, 'experts', ('dp', 'context'))
- in_second_new: float32 [2, 16, 1536, 1536], P(None, 'experts', ('dp', 'context'))
- down_new: float32 [2, 16, 768, 1536], P(None, 'experts', None, ('dp', 'context'))
- down_first_new: float32 [2, 16, 768, 1536], P(None, 'experts', None, ('dp', 'context'))
- down_second_new: float32 [2, 16, 768, 1536], P(None, 'experts', None, ('dp', 'context'))
- gains_new: float32 [2, 2, 1536], P(None, None, ('dp', 'context', 'experts'))
- gains_first_new: float32 [2, 2, 1536], P(None, None, ('dp', 'context', 'experts'))
- gains_second_new: float32 [2, 2, 1536], P(None, None, ('dp', 'context', 'experts'))
Inputs may be any that keep to these rules, and one draw needn't show every extreme that they name: `expert_ids`: each row names 4 different experts. In each layer, the 128 rows that one device holds (aligned blocks) name no expert more than 40 times; in some blocks an expert is named exactly 40 times. Each row is a permutation: the device at place c of context holds block block_order[s, c] of sequence s, tokens block_order[s, c] * 128 to block_order[s, c] * 128 + 127, and tokens, cotangent, expert_ids and gate_values store the blocks in that order. `qkv_second`: positive. `out_second`: positive. `in_second`: positive. `down_second`: positive. `gain_second`: positive.
All inputs are finite; a program needn't handle non-finite values.
Results may differ from a plain program's by a relative error of at most 0.024.
Values may be sent and summed in bfloat16 or wider, within the bound.
No kernel may reach another device: no remote copies, remote signals or barrier semaphores. Data moves between devices by JAX's collectives and lax.ppermute only.
A program may use at most 384 MiB of HBM per device.

v0:
```python
import jax
import jax.numpy as jnp
from jax import lax
from jax.sharding import PartitionSpec as P

D = 1536
HQ = 12
HK = 2
HD = 128
FF = 768
TOP = 4
LAYERS = 2
STEP = 5


beta_first = 0.9
beta_second = 0.95
adam_epsilon = 1e-08
gain_rate = 3.0
matrix_decay = 0.1
norm_epsilon = 1e-06
rope_base = 10000.0


def rope_angles(positions):
    half_size = HD // 2
    frequency = rope_base ** (jnp.arange(half_size, dtype=jnp.float32) * (-2.0 / HD))
    angles = positions.astype(jnp.float32)[:, None] * frequency[None, :]
    return (jnp.cos(angles), jnp.sin(angles))


def rotate(vectors, cosine_table, sine_table):
    half_size = vectors.shape[-1] // 2
    first_half = vectors[..., :half_size]
    second_half = vectors[..., half_size:]
    cosine_part = cosine_table[:, None, :]
    sine_part = sine_table[:, None, :]
    return jnp.concatenate(
        [
            first_half * cosine_part - second_half * sine_part,
            first_half * sine_part + second_half * cosine_part,
        ],
        axis=-1,
    )


def rope_back(gradient, cosine_table, sine_table):
    half_size = gradient.shape[-1] // 2
    first_half = gradient[..., :half_size]
    second_half = gradient[..., half_size:]
    cosine_part = cosine_table[:, None, :]
    sine_part = sine_table[:, None, :]
    return jnp.concatenate(
        [
            first_half * cosine_part + second_half * sine_part,
            second_half * cosine_part - first_half * sine_part,
        ],
        axis=-1,
    )


def slot_index(block_ids, experts_total, capacity):
    count_blocks = block_ids.shape[0]
    flat_ids = block_ids.reshape(count_blocks, -1)
    one_hot = (flat_ids[..., None] == jnp.arange(experts_total, dtype=jnp.int32)).astype(jnp.int32)
    earlier = jnp.cumsum(one_hot, axis=1) - one_hot
    rank_rows = jnp.sum(earlier * one_hot, axis=-1)
    block_base = jnp.arange(count_blocks, dtype=jnp.int32)[:, None] * (experts_total * capacity)
    return block_base + flat_ids * capacity + rank_rows


def exact_gelu(values):
    return jax.nn.gelu(values, approximate=False)


def norm_back(upstream, normed_rows, scale_rows, gain_row):
    scaled = upstream * gain_row
    return scale_rows * (
        scaled - normed_rows * jnp.mean(scaled * normed_rows, axis=-1, keepdims=True)
    )


def adam_update(weight, first_moment, second_moment, gradient, step_rate, decay_term):
    first_new = beta_first * first_moment + (1.0 - beta_first) * gradient
    second_new = beta_second * second_moment + (1.0 - beta_second) * gradient * gradient
    first_hat = first_new / (1.0 - beta_first**STEP)
    second_hat = second_new / (1.0 - beta_second**STEP)
    weight_new = weight - step_rate * (
        first_hat / (jnp.sqrt(second_hat) + adam_epsilon) + decay_term * weight
    )
    return (weight_new, first_new, second_new)


def local(
    tokens,
    cotangent,
    expert_ids,
    gate_values,
    block_order,
    qkv_weight,
    qkv_first,
    qkv_second,
    out_weight,
    out_first,
    out_second,
    in_weight,
    in_first,
    in_second,
    down_weight,
    down_first,
    down_second,
    norm_gains,
    gain_first,
    gain_second,
):
    low_qkv = qkv_weight.astype(jnp.bfloat16)
    low_out = out_weight.astype(jnp.bfloat16)
    low_gain = norm_gains.astype(jnp.bfloat16)
    qkv_full, out_full, gain_full = (
        lax.all_gather(low_qkv, ("dp", "context", "experts"), axis=1, tiled=True),
        lax.all_gather(low_out, ("dp", "context", "experts"), axis=2, tiled=True),
        lax.all_gather(low_gain, ("dp", "context", "experts"), axis=2, tiled=True),
    )
    in_full, down_full = (
        lax.all_gather(in_weight.astype(jnp.bfloat16), ("dp", "context"), axis=2, tiled=True),
        lax.all_gather(down_weight.astype(jnp.bfloat16), ("dp", "context"), axis=3, tiled=True),
    )
    token_rows = tokens.shape[1]
    context_count = lax.axis_size("context")
    order_row = block_order[0]
    own_block = jnp.sum(
        jnp.where(
            jnp.arange(context_count, dtype=jnp.int32) == lax.axis_index("context"), order_row, 0
        )
    )
    offsets = jnp.arange(token_rows, dtype=jnp.int32)
    query_pos = own_block * token_rows + offsets
    key_pos = (order_row[:, None] * token_rows + offsets[None, :]).reshape(-1)
    causal_mask = (query_pos[:, None] >= key_pos[None, :])[None, None]
    cosine_table, sine_table = rope_angles(query_pos)
    experts_total = in_full.shape[1] * lax.axis_size("experts")
    capacity = token_rows * TOP * 5 // (4 * experts_total)
    group_size = HQ // HK
    score_scale = HD ** (-0.5)
    query_width = HQ * HD
    key_width = HK * HD
    hidden_state = tokens[0].astype(jnp.float32)
    saved_layers = []
    for layer_index in range(LAYERS):
        gain_attn = gain_full[layer_index, 0].astype(jnp.float32)
        gain_ffn = gain_full[layer_index, 1].astype(jnp.float32)
        scale_one = lax.rsqrt(
            jnp.mean(hidden_state * hidden_state, axis=-1, keepdims=True) + norm_epsilon
        )
        normed_one = hidden_state * scale_one
        attn_in = (normed_one * gain_attn).astype(jnp.bfloat16)
        projected = jnp.dot(attn_in, qkv_full[layer_index], preferred_element_type=jnp.float32)
        query_rows = (
            rotate(projected[:, :query_width].reshape(-1, HQ, HD), cosine_table, sine_table)
            .astype(jnp.bfloat16)
            .reshape(-1, HK, group_size, HD)
        )
        key_rows = (
            rotate(
                projected[:, query_width : query_width + key_width].reshape(-1, HK, HD),
                cosine_table,
                sine_table,
            )
            .astype(jnp.bfloat16)
            .reshape(-1, key_width)
        )
        value_rows = projected[:, query_width + key_width :].astype(jnp.bfloat16)
        key_all, value_all = (
            lax.all_gather(key_rows, "context", axis=0, tiled=True),
            lax.all_gather(value_rows, "context", axis=0, tiled=True),
        )
        key_heads = key_all.reshape(-1, HK, HD)
        value_heads = value_all.reshape(-1, HK, HD)
        scores = (
            jnp.einsum("tkgd,skd->kgts", query_rows, key_heads, preferred_element_type=jnp.float32)
            * score_scale
        )
        scores = jnp.where(causal_mask, scores, -1e30)
        top_score = jnp.max(scores, axis=-1, keepdims=True)
        exp_scores = jnp.exp(scores - top_score)
        probs_full = exp_scores / jnp.sum(exp_scores, axis=-1, keepdims=True)
        probs_low = probs_full.astype(jnp.bfloat16)
        mixed_heads = (
            jnp.einsum("kgts,skd->tkgd", probs_low, value_heads, preferred_element_type=jnp.float32)
            .reshape(-1, query_width)
            .astype(jnp.bfloat16)
        )
        hidden_two = hidden_state + jnp.dot(
            mixed_heads, out_full[layer_index], preferred_element_type=jnp.float32
        )
        scale_two = lax.rsqrt(
            jnp.mean(hidden_two * hidden_two, axis=-1, keepdims=True) + norm_epsilon
        )
        normed_two = hidden_two * scale_two
        ffn_in = (normed_two * gain_ffn).astype(jnp.bfloat16)
        slot_rows = slot_index(expert_ids[layer_index, 0][None], experts_total, capacity).reshape(
            -1
        )
        gate_rows = gate_values[layer_index, 0]
        buffer_rows = (
            jnp.zeros((experts_total * capacity, D), jnp.bfloat16)
            .at[slot_rows]
            .set(jnp.repeat(ffn_in, TOP, axis=0))
        )
        received = lax.all_to_all(
            buffer_rows.reshape(experts_total, capacity, D),
            "experts",
            split_axis=0,
            concat_axis=1,
            tiled=True,
        )
        both_parts = jnp.einsum(
            "erd,edf->erf", received, in_full[layer_index], preferred_element_type=jnp.float32
        )
        gate_pre = both_parts[..., :FF]
        up_part = both_parts[..., FF:]
        activated = exact_gelu(gate_pre)
        hidden_rows = (activated * up_part).astype(jnp.bfloat16)
        returned = jnp.einsum(
            "erf,efd->erd", hidden_rows, down_full[layer_index], preferred_element_type=jnp.float32
        ).astype(jnp.bfloat16)
        came_back = lax.all_to_all(returned, "experts", split_axis=1, concat_axis=0, tiled=True)
        picked = came_back.reshape(-1, D)[slot_rows].reshape(-1, TOP, D).astype(jnp.float32)
        hidden_state = hidden_two + jnp.sum(gate_rows[..., None] * picked, axis=1)
        saved_layers.append(
            (
                scale_one,
                normed_one,
                attn_in,
                query_rows,
                key_heads,
                value_heads,
                probs_full,
                probs_low,
                mixed_heads,
                scale_two,
                normed_two,
                received,
                slot_rows,
                gate_rows,
                gate_pre,
                up_part,
                activated,
                hidden_rows,
            )
        )
    upstream = cotangent[0].astype(jnp.float32)
    qkv_grads = []
    out_grads = []
    in_grads = []
    down_grads = []
    gain_grads = []
    for layer_index in reversed(range(LAYERS)):
        (
            scale_one,
            normed_one,
            attn_in,
            query_rows,
            key_heads,
            value_heads,
            probs_full,
            probs_low,
            mixed_heads,
            scale_two,
            normed_two,
            received,
            slot_rows,
            gate_rows,
            gate_pre,
            up_part,
            activated,
            hidden_rows,
        ) = saved_layers[layer_index]
        gain_attn = gain_full[layer_index, 0].astype(jnp.float32)
        gain_ffn = gain_full[layer_index, 1].astype(jnp.float32)
        picks_grad = gate_rows[..., None] * upstream[:, None, :]
        grad_buffer = (
            jnp.zeros((experts_total * capacity, D), jnp.float32)
            .at[slot_rows]
            .set(picks_grad.reshape(-1, D))
            .astype(jnp.bfloat16)
        )
        owner_grad = lax.all_to_all(
            grad_buffer.reshape(experts_total, capacity, D),
            "experts",
            split_axis=0,
            concat_axis=1,
            tiled=True,
        )
        hidden_grad = jnp.einsum(
            "erd,efd->erf", owner_grad, down_full[layer_index], preferred_element_type=jnp.float32
        )
        down_grads.append(
            jnp.einsum("erf,erd->efd", hidden_rows, owner_grad, preferred_element_type=jnp.float32)
        )
        unused, gelu_back = jax.vjp(exact_gelu, gate_pre)
        gate_grad = gelu_back(hidden_grad * up_part)[0]
        both_grad = jnp.concatenate([gate_grad, hidden_grad * activated], axis=-1).astype(
            jnp.bfloat16
        )
        in_grads.append(
            jnp.einsum("erd,erf->edf", received, both_grad, preferred_element_type=jnp.float32)
        )
        rows_grad = jnp.einsum(
            "erf,edf->erd", both_grad, in_full[layer_index], preferred_element_type=jnp.float32
        )
        source_grad = lax.all_to_all(
            rows_grad.astype(jnp.bfloat16), "experts", split_axis=1, concat_axis=0, tiled=True
        ).astype(rows_grad.dtype)
        ffn_in_grad = jnp.sum(source_grad.reshape(-1, D)[slot_rows].reshape(-1, TOP, D), axis=1)
        gain_ffn_grad = jnp.sum(ffn_in_grad * normed_two, axis=0)
        upstream_two = upstream + norm_back(ffn_in_grad, normed_two, scale_two, gain_ffn)
        branch_grad = upstream_two.astype(jnp.bfloat16)
        out_grads.append(
            jnp.einsum("ti,td->id", mixed_heads, branch_grad, preferred_element_type=jnp.float32)
        )
        mixed_grad = (
            jnp.einsum(
                "td,id->ti", branch_grad, out_full[layer_index], preferred_element_type=jnp.float32
            )
            .astype(jnp.bfloat16)
            .reshape(-1, HK, group_size, HD)
        )
        probs_grad = jnp.einsum(
            "tkgd,skd->kgts", mixed_grad, value_heads, preferred_element_type=jnp.float32
        )
        row_delta = jnp.sum(probs_full * probs_grad, axis=-1, keepdims=True)
        scores_grad = (probs_full * (probs_grad - row_delta)).astype(jnp.bfloat16)
        query_grad = (
            jnp.einsum("kgts,skd->tkgd", scores_grad, key_heads, preferred_element_type=jnp.float32)
            * score_scale
        )
        key_term = (
            jnp.einsum(
                "kgts,tkgd->skd", scores_grad, query_rows, preferred_element_type=jnp.float32
            )
            * score_scale
        ).reshape(-1, key_width)
        value_term = jnp.einsum(
            "kgts,tkgd->skd", probs_low, mixed_grad, preferred_element_type=jnp.float32
        ).reshape(-1, key_width)
        key_grad, value_grad = (
            lax.psum_scatter(
                key_term.astype(jnp.bfloat16), "context", scatter_dimension=0, tiled=True
            ).astype(jnp.float32),
            lax.psum_scatter(
                value_term.astype(jnp.bfloat16), "context", scatter_dimension=0, tiled=True
            ).astype(jnp.float32),
        )
        projected_grad = jnp.concatenate(
            [
                rope_back(query_grad.reshape(-1, HQ, HD), cosine_table, sine_table).reshape(
                    -1, query_width
                ),
                rope_back(key_grad.reshape(-1, HK, HD), cosine_table, sine_table).reshape(
                    -1, key_width
                ),
                value_grad,
            ],
            axis=-1,
        ).astype(jnp.bfloat16)
        qkv_grads.append(
            jnp.einsum("td,tc->dc", attn_in, projected_grad, preferred_element_type=jnp.float32)
        )
        attn_in_grad = jnp.einsum(
            "tc,dc->td", projected_grad, qkv_full[layer_index], preferred_element_type=jnp.float32
        )
        gain_attn_grad = jnp.sum(attn_in_grad * normed_one, axis=0)
        upstream = upstream_two + norm_back(attn_in_grad, normed_one, scale_one, gain_attn)
        gain_grads.append(jnp.stack([gain_attn_grad, gain_ffn_grad]))
    qkv_local = jnp.stack(qkv_grads[::-1])
    out_local = jnp.stack(out_grads[::-1])
    gain_local = jnp.stack(gain_grads[::-1])
    in_local = jnp.stack(in_grads[::-1])
    down_local = jnp.stack(down_grads[::-1])
    qkv_sum, out_sum, gain_sum = (
        lax.psum_scatter(qkv_local, ("dp", "context", "experts"), scatter_dimension=1, tiled=True),
        lax.psum_scatter(out_local, ("dp", "context", "experts"), scatter_dimension=2, tiled=True),
        lax.psum_scatter(gain_local, ("dp", "context", "experts"), scatter_dimension=2, tiled=True),
    )
    in_sum, down_sum = (
        lax.psum_scatter(
            in_local.astype(jnp.bfloat16), ("dp", "context"), scatter_dimension=2, tiled=True
        ).astype(jnp.float32),
        lax.psum_scatter(
            down_local.astype(jnp.bfloat16), ("dp", "context"), scatter_dimension=3, tiled=True
        ).astype(jnp.float32),
    )
    wide_rate = 5.0 * D ** (-0.5)
    out_rate = 5.0 * (HQ * HD / 16.0) ** (-0.5)
    down_rate = 5.0 * (FF / 4.0) ** (-0.5)
    qkv_new, qkv_first_new, qkv_second_new = adam_update(
        qkv_weight, qkv_first, qkv_second, qkv_sum, wide_rate, matrix_decay
    )
    out_new, out_first_new, out_second_new = adam_update(
        out_weight, out_first, out_second, out_sum, out_rate, matrix_decay
    )
    in_new, in_first_new, in_second_new = adam_update(
        in_weight, in_first, in_second, in_sum, wide_rate, matrix_decay
    )
    down_new, down_first_new, down_second_new = adam_update(
        down_weight, down_first, down_second, down_sum, down_rate, matrix_decay
    )
    gains_new, gains_first_new, gains_second_new = adam_update(
        norm_gains, gain_first, gain_second, gain_sum, gain_rate, 0.0
    )
    return (
        hidden_state.astype(jnp.bfloat16)[None],
        upstream[None],
        qkv_new,
        qkv_first_new,
        qkv_second_new,
        out_new,
        out_first_new,
        out_second_new,
        in_new,
        in_first_new,
        in_second_new,
        down_new,
        down_first_new,
        down_second_new,
        gains_new,
        gains_first_new,
        gains_second_new,
    )


def solution(mesh):
    placed = (
        P(("dp", "experts"), "context", None),
        P(("dp", "experts"), "context", None),
        P(None, ("dp", "experts"), "context", None),
        P(None, ("dp", "experts"), "context", None),
        P(("dp", "experts"), None),
        P(None, ("dp", "context", "experts"), None),
        P(None, ("dp", "context", "experts"), None),
        P(None, ("dp", "context", "experts"), None),
        P(None, None, ("dp", "context", "experts")),
        P(None, None, ("dp", "context", "experts")),
        P(None, None, ("dp", "context", "experts")),
        P(None, "experts", ("dp", "context"), None),
        P(None, "experts", ("dp", "context"), None),
        P(None, "experts", ("dp", "context"), None),
        P(None, "experts", None, ("dp", "context")),
        P(None, "experts", None, ("dp", "context")),
        P(None, "experts", None, ("dp", "context")),
        P(None, None, ("dp", "context", "experts")),
        P(None, None, ("dp", "context", "experts")),
        P(None, None, ("dp", "context", "experts")),
    )
    return jax.shard_map(
        local,
        mesh=mesh,
        in_specs=placed,
        out_specs=(
            P(("dp", "experts"), "context", None),
            P(("dp", "experts"), "context", None),
            P(None, ("dp", "context", "experts"), None),
            P(None, ("dp", "context", "experts"), None),
            P(None, ("dp", "context", "experts"), None),
            P(None, None, ("dp", "context", "experts")),
            P(None, None, ("dp", "context", "experts")),
            P(None, None, ("dp", "context", "experts")),
            P(None, "experts", ("dp", "context"), None),
            P(None, "experts", ("dp", "context"), None),
            P(None, "experts", ("dp", "context"), None),
            P(None, "experts", None, ("dp", "context")),
            P(None, "experts", None, ("dp", "context")),
            P(None, "experts", None, ("dp", "context")),
            P(None, None, ("dp", "context", "experts")),
            P(None, None, ("dp", "context", "experts")),
            P(None, None, ("dp", "context", "experts")),
        ),
        check_vma=False,
    )
```

profile of v0, /device:TPU:1, one launch (start us, length us, event | category | flops | bytes accessed | tf_op | source)
XLA Modules:
  0.0 2377.3 jit_solution(2620374073049568716)
XLA Ops:
  19.6 376.1 %all_gather.27 = bf16[2,2,1536]{1,0,2:T(2,128)(2,1)S(1)} all-gather(bf16[2,2,12]{1,0,2:T(2,128)(2,1)S(1)} %copy.343), channel_id=1, replica_groups=mesh['dp'=2,'context'=8,'experts'=8] {'dp','context','experts'}, dimensions={2}, use_global_device_ids=true | all-gather | bytes 12384 | tf_op jit(solution)/shard_map/all_gather | solution.py:122
  396.9 27.5 %fusion.138 = (f32[1536]{0:T(1024)S(1)}, f32[1536]{0:T(1024)S(1)}, f32[1536]{0:T(1024)S(1)}, f32[1536]{0:T(1024)S(1)}) fusion(bf16[2,2,1536]{1,0,2:T(2,128)(2,1)S(1)} %all_gather.27), kind=kLoop, calls=%fused_computation.192 | loop fusion | flops 6144 | bytes 36864 | tf_op jit(solution)/shard_map/convert_element_type | solution.py:151
  424.5 19.1 fusion.194
  443.6 22.5 copy.464
  466.0 25.0 %fusion.192 = (bf16[1,1536,2048]{2,0,1:T(2,128)(2,1)}, bf16[1,1536,2048]{2,0,1:T(2,128)(2,1)S(1)}) fusion(bf16[2,1536,2048]{2,0,1:T(2,128)(2,1)} %all-gather.5.cloned.1.call-done), kind=kLoop, calls=%fused_computation.328 | loop fusion | bytes 25165824 | tf_op jit(solution)/shard_map/slice | solution.py:157
  501.1 29.0 %all_gather.29 = bf16[1024,256]{1,0:T(8,128)(2,1)S(1)} all-gather(bf16[128,256]{1,0:T(8,128)(2,1)S(1)} %slice.335), channel_id=1, replica_groups=mesh['dp'=2,'context'=8,'experts'=8] {'context'}, dimensions={0}, use_global_device_ids=true | all-gather | bytes 589824 | tf_op jit(solution)/shard_map/all_gather | solution.py:175
  530.3 27.0 %all_gather.30 = bf16[1024,256]{0,1:T(8,128)(2,1)S(1)} all-gather(bf16[128,256]{0,1:T(8,128)(2,1)S(1)} %bitcast.459), channel_id=1, replica_groups=mesh['dp'=2,'context'=8,'experts'=8] {'context'}, dimensions={0}, use_global_device_ids=true | all-gather | bytes 589824 | tf_op jit(solution)/shard_map/all_gather | solution.py:174
  587.4 12.5 copy.465
  647.3 22.5 copy.467
  700.9 27.0 %all_gather.35 = bf16[1024,256]{0,1:T(8,128)(2,1)S(1)} all-gather(bf16[128,256]{0,1:T(8,128)(2,1)S(1)} %bitcast.460), channel_id=1, replica_groups=mesh['dp'=2,'context'=8,'experts'=8] {'context'}, dimensions={0}, use_global_device_ids=true | all-gather | bytes 589824 | tf_op jit(solution)/shard_map/all_gather | solution.py:174
  727.9 30.6 %all_gather.34 = bf16[1024,256]{1,0:T(8,128)(2,1)S(1)} all-gather(bf16[128,256]{1,0:T(8,128)(2,1)S(1)} %slice.334), channel_id=1, replica_groups=mesh['dp'=2,'context'=8,'experts'=8] {'context'}, dimensions={0}, use_global_device_ids=true | all-gather | bytes 589824 | tf_op jit(solution)/shard_map/all_gather | solution.py:175
  783.5 12.4 copy.468
  907.3 80.1 %reduce-scatter.17.cloned.1.call-done = bf16[128,256]{1,0:T(8,128)(2,1)} async-done(((bf16[1024,256]{1,0:T(8,128)(2,1)}), bf16[128,256]{1,0:T(8,128)(2,1)}) %reduce-scatter.17.cloned.1.call-update) | async-done | bytes 65552
  989.1 72.1 %reduce-scatter.19.cloned.1.call-done = bf16[128,256]{1,0:T(8,128)(2,1)} async-done(((bf16[1024,256]{1,0:T(8,128)(2,1)}), bf16[128,256]{1,0:T(8,128)(2,1)}) %reduce-scatter.19.cloned.1.call-update) | async-done | bytes 65552
  1086.0 27.3 %all_to_all.120 = bf16[16,40,1536]{2,1,0:T(8,128)(2,1)S(1)} all-to-all(bf16[16,40,1536]{2,1,0:T(8,128)(2,1)S(1)} %bitcast.398), channel_id=1, replica_groups=mesh['dp'=2,'context'=8,'experts'=8] {'experts'}, dimensions={0} | all-to-all | bytes 3932160 | tf_op jit(solution)/shard_map/all_to_all | solution.py:288
  1128.2 25.2 %all_to_all.121 = bf16[2,320,1536]{2,0,1:T(2,128)(2,1)S(1)} all-to-all(bf16[2,320,1536]{2,0,1:T(2,128)(2,1)S(1)} %copy.401), channel_id=1, replica_groups=mesh['dp'=2,'context'=8,'experts'=8] {'experts'}, dimensions={1} | all-to-all | bytes 3932160 | tf_op jit(solution)/shard_map/all_to_all | solution.py:312
  1211.2 24.1 %copy.415 = bf16[2,2,768,1536]{2,1,0,3:T(2,128)(2,1)} copy(bf16[2,2,768,1536]{3,2,1,0:T(8,128)(2,1)} %pad_maximum_fusion.3) | data formatting | bytes 18874368 | tf_op jit(solution)/shard_map/stack | solution.py:380
  1246.2 28.4 %copy.414 = f32[2,1536,1536]{1,0,2:T(2,128)} copy(f32[2,1536,1536]{2,1,0:T(8,128)} %pad_maximum_fusion.1) | data formatting | bytes 37748736 | tf_op jit(solution)/shard_map/stack | solution.py:377
  1286.0 41.9 %reduce-scatter.23.cloned.1.call-done = bf16[128,256]{1,0:T(8,128)(2,1)} async-done(((bf16[1024,256]{1,0:T(8,128)(2,1)}), bf16[128,256]{1,0:T(8,128)(2,1)}) %reduce-scatter.23.cloned.1.call-update) | async-done | bytes 65552
  1342.1 41.8 %copy.413 = f32[2,1536,2048]{2,0,1:T(2,128)} copy(f32[2,1536,2048]{2,1,0:T(8,128)} %pad_maximum_fusion) | data formatting | bytes 50331648 | tf_op jit(solution)/shard_map/stack | solution.py:376
  1416.7 325.2 %all-reduce.3 = f32[2,2,1536]{2,1,0:T(2,128)S(1)} all-reduce(f32[2,2,1536]{2,1,0:T(2,128)S(1)} %pad_maximum_fusion.24), channel_id=10, replica_groups=mesh['dp'=2,'context'=8,'experts'=8] {'dp','context','experts'}, use_global_device_ids=true, to_apply=%region_41.42.clone | all-reduce | flops 6144 | bytes 49152
  1749.0 216.4 %all-reduce.10.cloned.1.call-done = f32[2,1536,1536]{1,0,2:T(2,128)} async-done(((f32[2,1536,1536]{1,0,2:T(2,128)}), f32[2,1536,1536]{1,0,2:T(2,128)}) %all-reduce.10.cloned.1.call-update) | async-done | bytes 18874384
  1967.7 233.7 %all-reduce.8.cloned.1.call-done = f32[2,1536,2048]{2,0,1:T(2,128)} async-done(((f32[2,1536,2048]{2,0,1:T(2,128)}), f32[2,1536,2048]{2,0,1:T(2,128)}) %all-reduce.8.cloned.1.call-update) | async-done | bytes 25165840
  2204.1 159.1 %reduce-scatter.15.cloned.1.call-done = bf16[2,2,96,1536]{3,2,1,0:T(8,128)(2,1)} async-done(((bf16[2,2,1536,1536]{3,2,1,0:T(8,128)(2,1)}), bf16[2,2,96,1536]{3,2,1,0:T(8,128)(2,1)}) %reduce-scatter.15.cloned.1.call-update) | async-done | bytes 1179664 | tf_op jit(solution)/shard_map/reduce_scatter | solution.py:387
  (554 shorter events, 453.0 us)
Async XLA Ops:
  7.2 417.3 %all-gather.7.cloned.1.call-start = ((), (), s32[]{:S(2)}) async-start(), calls=%async_computation.14 | async-start | bytes 9510912 | tf_op jit(solution)/shard_map/all_gather | solution.py:121
  9.0 457.0 %all-gather.5.cloned.1.call-start = ((), (), s32[]{:S(2)}) async-start(), calls=%async_computation.13 | async-start | bytes 12681216 | tf_op jit(solution)/shard_map/all_gather | solution.py:120
  10.7 567.4 %all-gather.11.cloned.1.call-start = ((), (), s32[]{:S(2)}) async-start(), calls=%async_computation.16 | async-start | bytes 10027008 | tf_op jit(solution)/shard_map/all_gather | solution.py:126
  13.8 587.5 %all-gather.9.cloned.1.call-start = ((), (), s32[]{:S(2)}) async-start(), calls=%async_computation.15 | async-start | bytes 20054016 | tf_op jit(solution)/shard_map/all_gather | solution.py:125
  15.0 380.8 %copy-start.19 = (bf16[1,128,1536]{2,1,0:T(8,128)(2,1)S(1)}, bf16[1,128,1536]{2,1,0:T(8,128)(2,1)}, u32[]{:S(2)}) copy-start(bf16[1,128,1536]{2,1,0:T(8,128)(2,1)} %param.20) | copy-start | bytes 1179652
  16.7 682.8 %copy-start.55 = (f32[128,64]{0,1:T(8,128)}, f32[128,64]{0,1:T(8,128)S(1)}, u32[]{:S(2)}) copy-start(f32[128,64]{0,1:T(8,128)S(1)} %get-tuple-element.158) | copy-start | bytes 98308
  16.7 682.8 %copy-start.58 = (f32[128,64]{0,1:T(8,128)}, f32[128,64]{0,1:T(8,128)S(1)}, u32[]{:S(2)}) copy-start(f32[128,64]{0,1:T(8,128)S(1)} %get-tuple-element.159) | copy-start | bytes 98308
  16.8 683.4 %copy-start.37 = (f32[128,64]{1,0:T(8,128)}, f32[128,64]{1,0:T(8,128)S(1)}, u32[]{:S(2)}) copy-start(f32[128,64]{1,0:T(8,128)S(1)} %copy.345) | copy-start | bytes 98308
  17.0 683.3 %copy-start.40 = (f32[128,64]{1,0:T(8,128)}, f32[128,64]{1,0:T(8,128)S(1)}, u32[]{:S(2)}) copy-start(f32[128,64]{1,0:T(8,128)S(1)} %copy.346) | copy-start | bytes 98308
  574.5 25.4 %all-to-all-start = ((bf16[16,40,1536]{2,1,0:T(8,128)(2,1)}), bf16[16,40,1536]{2,1,0:T(8,128)(2,1)S(1)}, u32[]{:S(2)}, u32[]{:S(2)}) async-start(bf16[16,40,1536]{2,1,0:T(8,128)(2,1)} %bitcast.396), calls=%async_computation | async-start | bytes 3932160 | tf_op jit(solution)/shard_map/all_to_all | solution.py:210
  617.9 51.8 %all-to-all-start.1 = ((bf16[2,320,1536]{2,0,1:T(2,128)(2,1)}), bf16[2,320,1536]{2,0,1:T(2,128)(2,1)S(1)}, u32[]{:S(2)}, u32[]{:S(2)}) async-start(bf16[2,320,1536]{2,0,1:T(2,128)(2,1)} %copy.364), calls=%async_computation.1 | async-start | bytes 3932160 | tf_op jit(solution)/shard_map/all_to_all | solution.py:227
  671.1 104.0 %all-to-all-start.4 = ((bf16[16,40,1536]{2,1,0:T(8,128)(2,1)}), bf16[16,40,1536]{2,1,0:T(8,128)(2,1)}, u32[]{:S(2)}, u32[]{:S(2)}) async-start(bf16[16,40,1536]{2,1,0:T(8,128)(2,1)} %bitcast.67), calls=%async_computation.4 | async-start | bytes 3932160 | tf_op jit(solution)/shard_map/all_to_all | solution.py:288
  775.1 20.9 all-to-all-start.2
  816.5 19.5 all-to-all-start.3
  837.3 23.4 all-to-all-start.5
  841.6 145.8 %reduce-scatter.17.cloned.1.call-start = ((), (), s32[]{:S(2)}) async-start(), calls=%async_computation.18 | async-start | bytes 589824
  895.4 165.8 %reduce-scatter.19.cloned.1.call-start = ((), (), s32[]{:S(2)}) async-start(), calls=%async_computation.19 | async-start | bytes 589824
  905.2 379.0 %reduce-scatter.21.cloned.1.call-start = ((), (), s32[]{:S(2)}) async-start(), calls=%async_computation.20 | async-start | bytes 589824
  1184.2 143.7 %reduce-scatter.23.cloned.1.call-start = ((), (), s32[]{:S(2)}) async-start(), calls=%async_computation.21 | async-start | bytes 589824
  1191.0 553.9 %all-reduce.12.cloned.1.call-start = ((), (), s32[]{:S(2)}) async-start(), calls=%async_computation.24 | async-start | bytes 18874368
  1235.3 730.1 %all-reduce.10.cloned.1.call-start = ((), (), s32[]{:S(2)}) async-start(), calls=%async_computation.23 | async-start | bytes 37748736
  1274.7 926.7 %all-reduce.8.cloned.1.call-start = ((), (), s32[]{:S(2)}) async-start(), calls=%async_computation.22 | async-start | bytes 50331648
  1383.9 979.3 %reduce-scatter.15.cloned.1.call-start = ((), (), s32[]{:S(2)}) async-start(), calls=%async_computation.17 | async-start | bytes 20054016 | tf_op jit(solution)/shard_map/reduce_scatter | solution.py:387
  1749.0 614.3 %copy-start.14 = (f32[2,2,96,1536]{3,2,1,0:T(8,128)S(1)}, f32[2,2,96,1536]{3,2,1,0:T(8,128)}, u32[]{:S(2)}) copy-start(f32[2,2,96,1536]{3,2,1,0:T(8,128)} %param.31) | copy-start | bytes 7077892
  (137 other events, 3882.1 us)
Sparse Core Ops, SparseCore 0:
  11.6 74.5 all-gather.6
  89.9 71.1 all-gather.4
  164.2 76.9 all-gather.10
  244.2 116.9 all-gather.8
  895.5 91.8 reduce-scatter.16
  991.8 69.3 reduce-scatter.18
  1184.3 70.0 reduce-scatter.20
  1258.3 69.5 reduce-scatter.22
  1330.4 409.7 all-reduce.11
  1745.4 219.8 all-reduce.9
  1971.5 229.8 all-reduce.7
  2206.2 156.9 reduce-scatter.14
where the time goes:
time: 2390 us; the launch traced here: 2380 us
  blocking collectives  867 us (36%)
  waiting for transfers between devices  818 us (34%)
  local copies, waits for them, and re-layouts  350 us (15%)
  matrix products  158 us (7%)
  other arithmetic  134 us (6%)
  starting transfers between devices  31 us (1%)
    unnamed x19, waiting for transfers between devices  644 us
    all_gather x1, blocking collectives, local(): lax.all_gather(low_gain, ('dp', 'context', 'experts'), axis=2, tiled=True)  376 us
    unnamed x1, blocking collectives  325 us
    reduce_scatter x1, waiting for transfers between devices, local(): lax.psum_scatter(in_local.astype(jnp.bfloat16), ('dp', 'context'), scatte...  159 us
    unnamed x303, local copies, waits for them, and re-layouts  110 us
    all_gather x2, blocking collectives, local(): lax.all_gather(value_rows, 'context', axis=0, tiled=True)  59.6 us
    all_gather x2, blocking collectives, local(): lax.all_gather(key_rows, 'context', axis=0, tiled=True)  53.9 us
  transfers between devices with their start and end apart: 18, of which 8 were waited for; matrix products, arithmetic and copies ran while one was open for 20% of the time, Pallas kernels for 0%

commit v1 on v0

v1 whole, which is shorter than its diff:
```python
import functools
import itertools
import jax
import jax.numpy as jnp
from jax import lax
from jax.experimental import pallas as pl
from jax.experimental.pallas import tpu as pltpu
from jax.sharding import PartitionSpec as P

D = 1536
HQ = 12
HK = 2
HD = 128
FF = 768
TOP = 4
LAYERS = 2
STEP = 5
EXPERTS = 16
CAP = 40
ROWS = EXPERTS * CAP
QKV = (HQ + 2 * HK) * HD
QW = HQ * HD
KW = HK * HD
YQ = QKV // 4
YO = QW // 4
TOK = 128
KEYS = 1024
GROUP = HQ // HK
GT = GROUP * TOK
score_scale = HD ** (-0.5)
norm_epsilon = 1e-06
BF = jnp.bfloat16
F32 = jnp.float32
MIB = 1 << 20


def dot(a, b, contract):
    return lax.dot_general(a, b, (contract, ((), ())), preferred_element_type=F32)


NN = ((1,), (0,))
NT = ((1,), (1,))
TN = ((0,), (0,))


def split(value):
    high = value.astype(BF)
    return high, (value - high.astype(F32)).astype(BF)


def whole():
    return pl.BlockSpec(memory_space=pltpu.VMEM)


def scalars():
    return pl.BlockSpec(memory_space=pltpu.SMEM)


def anywhere():
    return pl.BlockSpec(memory_space=pl.ANY)


def call(body, outs, ins, specs, scratch, flops, moved, name, mib=40, out_specs=None, grid=None):
    return pl.pallas_call(
        body,
        out_shape=[jax.ShapeDtypeStruct(s, t) for s, t in outs],
        in_specs=specs,
        out_specs=out_specs or [whole() for _ in outs],
        scratch_shapes=scratch,
        grid=grid or (),
        compiler_params=pltpu.CompilerParams(vmem_limit_bytes=mib * MIB),
        cost_estimate=pl.CostEstimate(flops=int(flops), bytes_accessed=int(moved), transcendentals=0),
        name=name,
    )(*ins)


def turn(head, cosine, sine):
    return head * cosine + pltpu.roll(head, HD // 2, 1) * sine


def rope_heads(part, y, cosine, sine):
    heads = []
    for i in range(4):
        head = part[:, i * HD : (i + 1) * HD]
        heads.append(head if y == 3 and i >= 2 else turn(head, cosine, sine))
    return jnp.concatenate(heads, axis=1)


def load_parts(w_ref, buf, sem, column, width):
    copies = [
        pltpu.make_async_copy(w_ref.at[:, y, :, pl.ds(column, width)], buf.at[y], sem.at[y])
        for y in range(4)
    ]
    for copy in copies:
        copy.start()
    return copies


def project_body(add, *refs):
    if add:
        (base, came, high, low, gain, cosine, sine, w, hidden, attn_in, scale, out, buf, sem) = refs
    else:
        (base, gain, cosine, sine, w, attn_in, scale, out, buf, sem) = refs
    copies = load_parts(w, buf, sem, 0, YQ)
    h = base[...].astype(F32)
    if add:
        rows = came[...]
        h = h + (dot(high[...], rows, NN) + dot(low[...], rows, NN))
        hidden[...] = h
    factor = lax.rsqrt(jnp.mean(h * h, axis=1, keepdims=True) + norm_epsilon)
    scale[...] = factor
    fed = (h * factor * gain[...]).astype(BF)
    attn_in[...] = fed
    for y in range(4):
        copies[y].wait()
        part = dot(fed, buf[y].reshape(D, YQ), NN)
        out[:, y * YQ : (y + 1) * YQ] = rope_heads(part, y, cosine[...], sine[...]).astype(BF)


def project(base, gain, cosine, sine, w, extra=None):
    ins = [base] + list(extra or ()) + [gain, cosine, sine, w]
    outs = [((TOK, D), BF), ((TOK, 1), F32), ((TOK, QKV), BF)]
    if extra:
        outs = [((TOK, D), F32)] + outs
    return call(
        functools.partial(project_body, bool(extra)),
        outs,
        ins,
        [whole() for _ in ins[:-1]] + [anywhere()],
        [pltpu.VMEM((4, 32, 48, YQ), BF), pltpu.SemaphoreType.DMA((4,))],
        2 * TOK * D * QKV,
        2 * D * QKV + 8 * TOK * D,
        "project",
    )


def keep_keys(kv_refs, buf):
    for k, ref in enumerate(kv_refs):
        for h in range(2):
            buf[(2 * k + h) * TOK : (2 * k + h + 1) * TOK, :] = ref[h]


def stack_heads(ref, j):
    return jnp.concatenate(
        [ref[:, (j * GROUP + i) * HD : (j * GROUP + i + 1) * HD] for i in range(GROUP)], axis=0
    )


def unstack(total):
    return jnp.concatenate(
        [total[:, i * TOK : (i + 1) * TOK].T for i in range(GROUP)], axis=1
    )


def attend_body(qkv, kv0, kv1, kv2, kv3, key_pos, query_pos, mixed, norm, buf, keep):
    keep_keys((kv0, kv1, kv2, kv3), buf)
    places = jnp.concatenate([query_pos[...]] * GROUP, axis=1)
    for j in range(HK):
        queries = stack_heads(qkv, j)

        def score(b, top):
            at = pl.ds(pl.multiple_of(b * TOK, TOK), TOK)
            keys = buf[at, j * HD : (j + 1) * HD]
            values = dot(keys, queries, NT) * score_scale
            values = jnp.where(key_pos[at, :] <= places, values, -1e30)
            keep[at, :] = values
            return jnp.maximum(top, jnp.max(values, axis=0, keepdims=True))

        top = lax.fori_loop(0, KEYS // TOK, score, jnp.full((1, GT), -1e30, F32))

        def mix(b, carry):
            total, share = carry
            at = pl.ds(pl.multiple_of(b * TOK, TOK), TOK)
            e = jnp.exp(keep[at, :] - top)
            values = buf[at, KW + j * HD : KW + (j + 1) * HD]
            share = share + jnp.sum(e, axis=0, keepdims=True)
            return total + dot(values, e.astype(BF), TN), share

        total, share = lax.fori_loop(
            0, KEYS // TOK, mix, (jnp.zeros((HD, GT), F32), jnp.zeros((1, GT), F32))
        )
        norm[j : j + 1, :] = top + jnp.log(share)
        mixed[:, j * GT : (j + 1) * GT] = unstack(total / share).astype(BF)


def attend(qkv, kv, key_pos, query_pos):
    ins = [qkv, *kv, key_pos, query_pos]
    return call(
        attend_body,
        [((TOK, QW), BF), ((HK, GT), F32)],
        ins,
        [whole() for _ in ins],
        [pltpu.VMEM((KEYS, 2 * KW), BF), pltpu.VMEM((KEYS, GT), F32)],
        4 * TOK * KEYS * QW,
        2 * KEYS * 2 * KW,
        "attend",
    )


def attend_back_body(
    qkv, kv0, kv1, kv2, kv3, key_pos, query_pos, norm, d_mixed, d_queries, d_pairs, buf, kept, given
):
    keep_keys((kv0, kv1, kv2, kv3), buf)
    places = jnp.concatenate([query_pos[...]] * GROUP, axis=1)
    for j in range(HK):
        queries = stack_heads(qkv, j)
        upstream = stack_heads(d_mixed, j)
        level = norm[j : j + 1, :]

        def probs(b, delta):
            at = pl.ds(pl.multiple_of(b * TOK, TOK), TOK)
            keys = buf[at, j * HD : (j + 1) * HD]
            values = buf[at, KW + j * HD : KW + (j + 1) * HD]
            scores = dot(keys, queries, NT) * score_scale
            p = jnp.where(key_pos[at, :] <= places, jnp.exp(scores - level), 0.0)
            dp = dot(values, upstream, NT)
            kept[at, :] = p
            given[at, :] = dp
            d_pairs[at, KW + j * HD : KW + (j + 1) * HD] = dot(p.astype(BF), upstream, NN).astype(BF)
            return delta + jnp.sum(p * dp, axis=0, keepdims=True)

        delta = lax.fori_loop(0, KEYS // TOK, probs, jnp.zeros((1, GT), F32))

        def back(b, total):
            at = pl.ds(pl.multiple_of(b * TOK, TOK), TOK)
            keys = buf[at, j * HD : (j + 1) * HD]
            ds = (kept[at, :] * (given[at, :] - delta)).astype(BF)
            d_pairs[at, j * HD : (j + 1) * HD] = (dot(ds, queries, NN) * score_scale).astype(BF)
            return total + dot(keys, ds, TN)

        total = lax.fori_loop(0, KEYS // TOK, back, jnp.zeros((HD, GT), F32))
        d_queries[:, j * GT : (j + 1) * GT] = unstack(total * score_scale)


def attend_back(qkv, kv, key_pos, query_pos, norm, d_mixed):
    ins = [qkv, *kv, key_pos, query_pos, norm, d_mixed]
    return call(
        attend_back_body,
        [((TOK, QW), F32), ((KEYS, 2 * KW), BF)],
        ins,
        [whole() for _ in ins],
        [pltpu.VMEM((KEYS, 2 * KW), BF), pltpu.VMEM((KEYS, GT), F32), pltpu.VMEM((KEYS, GT), F32)],
        10 * TOK * KEYS * QW,
        4 * KEYS * 2 * KW,
        "attend_back",
    )


def branch_body(base, mixed, gain, pick, w, hidden, scale, sent, buf, sem):
    copies = load_parts(w, buf, sem, YQ, YO)
    total = base[...].astype(F32)
    for y in range(4):
        copies[y].wait()
        total = total + dot(mixed[:, y * YO : (y + 1) * YO], buf[y].reshape(D, YO), NT)
    hidden[...] = total
    factor = lax.rsqrt(jnp.mean(total * total, axis=1, keepdims=True) + norm_epsilon)
    scale[...] = factor
    fed = (total * factor * gain[...]).astype(BF)
    sent[...] = dot(pick[...], fed, NN).astype(BF)


def branch(base, mixed, gain, pick, w):
    ins = [base, mixed, gain, pick, w]
    return call(
        branch_body,
        [((TOK, D), F32), ((TOK, 1), F32), ((ROWS, D), BF)],
        ins,
        [whole() for _ in ins[:-1]] + [anywhere()],
        [pltpu.VMEM((4, 32, 48, YO), BF), pltpu.SemaphoreType.DMA((4,))],
        2 * TOK * D * QW + 2 * TOK * D * ROWS,
        2 * D * QW + 2 * ROWS * D,
        "branch",
    )


BLOCK = 320


def load_expert(w_refs, places, buf, sem):
    copies = []
    for ref in w_refs:
        lead = ref.shape[:-2]
        for at in itertools.product(*[range(n) for n in lead]):
            row = pl.multiple_of(places[len(copies)] * 96, 96)
            copies.append(
                pltpu.make_async_copy(
                    ref.at[at] if at else ref, buf.at[pl.ds(row, 96), :], sem.at[len(copies)]
                )
            )
    for copy in copies:
        copy.start()
    for copy in copies:
        copy.wait()


def gelu_parts(x):
    cdf = 0.5 * (1.0 + lax.erf(x * (0.5**0.5)))
    density = jnp.exp(-0.5 * x * x) * 0.3989422804014327
    return x * cdf, cdf + x * density


def ffn_body(n, places, received, *refs):
    w_refs, (returned, hidden, act, slope, buf, sem) = refs[:n], refs[n:]

    @pl.when(pl.program_id(0) == 0)
    def _():
        load_expert(w_refs, places, buf, sem)

    both = dot(received[...], buf[:, : 2 * FF], NN)
    up = both[:, FF:]
    gelu, gelu_slope = gelu_parts(both[:, :FF])
    low = (gelu * up).astype(BF)
    hidden[...] = low
    act[...] = gelu
    slope[...] = gelu_slope * up
    returned[...] = dot(low, buf[:, 2 * FF :], NT).astype(BF)


def row_block(width):
    return pl.BlockSpec((BLOCK, width), lambda i: (i, 0))


def ffn(received, w_list, places):
    return call(
        functools.partial(ffn_body, len(w_list)),
        [((ROWS, D), BF), ((ROWS, FF), BF), ((ROWS, FF), F32), ((ROWS, FF), F32)],
        [places, received, *w_list],
        [scalars(), row_block(D)] + [anywhere() for _ in w_list],
        [pltpu.VMEM((D, 3 * FF), BF), pltpu.SemaphoreType.DMA((16,))],
        2 * ROWS * D * 3 * FF,
        2 * D * 3 * FF + 16 * ROWS * FF,
        "ffn",
        out_specs=[row_block(D), row_block(FF), row_block(FF), row_block(FF)],
        grid=(ROWS // BLOCK,),
    )


def ffn_back_body(n, places, owner, act, slope, *refs):
    w_refs, (d_rows, d_both, buf, sem) = refs[:n], refs[n:]

    @pl.when(pl.program_id(0) == 0)
    def _():
        load_expert(w_refs, places, buf, sem)

    d_hidden = dot(owner[...], buf[:, 2 * FF :], NN)
    both = jnp.concatenate([d_hidden * slope[...], d_hidden * act[...]], axis=1).astype(BF)
    d_both[...] = both
    d_rows[...] = dot(both, buf[:, : 2 * FF], NT).astype(BF)


def ffn_back(owner, act, slope, w_list, places):
    return call(
        functools.partial(ffn_back_body, len(w_list)),
        [((ROWS, D), BF), ((ROWS, 2 * FF), BF)],
        [places, owner, act, slope, *w_list],
        [scalars(), row_block(D), row_block(FF), row_block(FF)] + [anywhere() for _ in w_list],
        [pltpu.VMEM((D, 3 * FF), BF), pltpu.SemaphoreType.DMA((16,))],
        2 * ROWS * D * 3 * FF,
        2 * D * 3 * FF + 16 * ROWS * FF,
        "ffn_back",
        out_specs=[row_block(D), row_block(2 * FF)],
        grid=(ROWS // BLOCK,),
    )


def ffn_grad_body(received, d_both, owner, hidden, out):
    out[:, 0, :, : 2 * FF] = dot(received[...], d_both[...], TN).astype(BF).reshape(8, 96, 2 * FF)
    out[:, 0, :, 2 * FF :] = dot(owner[...], hidden[...], TN).astype(BF).reshape(8, 96, FF)


def ffn_grad(received, d_both, owner, hidden):
    half = pl.BlockSpec((ROWS, D // 2), lambda i: (0, i))
    fixed = lambda width: pl.BlockSpec((ROWS, width), lambda i: (0, 0))
    return call(
        ffn_grad_body,
        [((8, 2, 96, 3 * FF), BF)],
        [received, d_both, owner, hidden],
        [half, fixed(2 * FF), half, fixed(FF)],
        [],
        2 * ROWS * D * 3 * FF,
        2 * D * 3 * FF + 8 * ROWS * D,
        "ffn_grad",
        out_specs=[pl.BlockSpec((8, 1, 96, 3 * FF), lambda i: (0, i, 0, 0))],
        grid=(2,),
    )[0]


def norm_back(upstream, rows, factor, gain):
    normed = rows * factor
    scaled = upstream * gain
    return (
        factor * (scaled - normed * jnp.mean(scaled * normed, axis=1, keepdims=True)),
        jnp.sum(upstream * normed, axis=0, keepdims=True),
    )


def branch_back_body(source, pick_t, base, scale, gain, d_out, w, d_base, low, d_mixed, d_gain, buf, sem):
    copies = load_parts(w, buf, sem, YQ, YO)
    d_fed = dot(pick_t[...], source[...], NN)
    term, d_gain[...] = norm_back(d_fed, base[...], scale[...], gain[...])
    total = d_out[...].astype(F32) + term
    d_base[...] = total
    rounded = total.astype(BF)
    low[...] = rounded
    for y in range(4):
        copies[y].wait()
        d_mixed[:, y * YO : (y + 1) * YO] = dot(rounded, buf[y].reshape(D, YO), NN).astype(BF)


def branch_back(source, pick_t, base, scale, gain, d_out, w):
    ins = [source, pick_t, base, scale, gain, d_out, w]
    return call(
        branch_back_body,
        [((TOK, D), F32), ((TOK, D), BF), ((TOK, QW), BF), ((1, D), F32)],
        ins,
        [whole() for _ in ins[:-1]] + [anywhere()],
        [pltpu.VMEM((4, 32, 48, YO), BF), pltpu.SemaphoreType.DMA((4,))],
        2 * TOK * D * QW + 2 * TOK * D * ROWS,
        2 * D * QW + 2 * ROWS * D,
        "branch_back",
    )


def project_back_body(last, *refs):
    if last:
        (dq, dkv, cosine, sine, base, scale, gain, d_out, w, d_base, d_proj, d_gain, buf, sem) = refs
    else:
        (dq, dkv, cosine, sine, base, scale, gain, d_out, pick, gate, w) = refs[:11]
        (d_base, d_proj, d_gain, sent, buf, sem) = refs[11:]
    copies = load_parts(w, buf, sem, 0, YQ)
    total = jnp.zeros((TOK, D), F32)
    for y in range(4):
        part = dq[:, y * YQ : (y + 1) * YQ] if y < 3 else dkv[...]
        rounded = rope_heads(part, y, cosine[...], -sine[...]).astype(BF)
        d_proj[:, y * YQ : (y + 1) * YQ] = rounded
        copies[y].wait()
        total = total + dot(rounded, buf[y].reshape(D, YQ), NT)
    term, d_gain[...] = norm_back(total, base[...].astype(F32), scale[...], gain[...])
    d_hidden = d_out[...] + term
    d_base[...] = d_hidden
    if not last:
        high, low = split(d_hidden)
        rows = dot(pick[...], high, NN) + dot(pick[...], low, NN)
        sent[...] = (rows * gate[...]).astype(BF)


def project_back(dq, dkv, cosine, sine, base, scale, gain, d_out, w, extra=None):
    ins = [dq, dkv, cosine, sine, base, scale, gain, d_out] + list(extra or ()) + [w]
    outs = [((TOK, D), F32), ((TOK, QKV), BF), ((1, D), F32)]
    if extra:
        outs = outs + [((ROWS, D), BF)]
    return call(
        functools.partial(project_back_body, not extra),
        outs,
        ins,
        [whole() for _ in ins[:-1]] + [anywhere()],
        [pltpu.VMEM((4, 32, 48, YQ), BF), pltpu.SemaphoreType.DMA((4,))],
        2 * TOK * D * QKV,
        2 * D * QKV + 8 * TOK * D,
        "project_back",
    )


def wide_grad_body(core, one, two, three, four, out):
    del core
    out[0, 0, :, :YQ] = dot(one[...], two[...], TN).astype(BF)
    out[0, 0, :, YQ:] = dot(three[...], four[...], TN).astype(BF)


def half_of(rows):
    return pl.BlockSpec((rows, D // 2), lambda i, y, core: (0, (i + core[0]) % 2))


def wide_grad(core, attn_in, d_projected, d_branch, mixed):
    return pl.pallas_call(
        wide_grad_body,
        out_shape=jax.ShapeDtypeStruct((2, 4, D // 2, YQ + YO), BF),
        grid_spec=pltpu.PrefetchScalarGridSpec(
            num_scalar_prefetch=1,
            grid=(2, 4),
            in_specs=[
                half_of(TOK),
                pl.BlockSpec((TOK, YQ), lambda i, y, core: (0, y)),
                half_of(TOK),
                pl.BlockSpec((TOK, YO), lambda i, y, core: (0, y)),
            ],
            out_specs=pl.BlockSpec((1, 1, D // 2, YQ + YO), lambda i, y, core: (i, y, 0, 0)),
        ),
        compiler_params=pltpu.CompilerParams(vmem_limit_bytes=40 * MIB),
        cost_estimate=pl.CostEstimate(
            flops=2 * TOK * D * (QKV + QW), bytes_accessed=2 * D * (QKV + QW), transcendentals=0
        ),
        name="wide_grad",
    )(core, attn_in, d_projected, d_branch, mixed)


def spread_matrices():
    row = jnp.arange(384, dtype=jnp.int32)[:, None]
    column = jnp.arange(768, dtype=jnp.int32)[None, :]
    place = (column // 24) * 12 + column % 12
    late = (column % 24) // 12
    return jnp.stack([((row == place) & (late == h)).astype(BF) for h in range(2)])


def owner_grad_body(core, left, right, spread, out):
    del core
    width = right.shape[1] // 2
    rows = left[...]
    both = jnp.concatenate([dot(rows, spread[h], NN).astype(BF) for h in range(2)], axis=0)
    sides = jnp.concatenate([right[:, :width], right[:, width:]], axis=0)
    out[0] = dot(both, sides, TN).astype(BF).reshape(32, 24, width)


def owner_grad(core, left, right, spread):
    width = right.shape[1] // 2
    return pl.pallas_call(
        owner_grad_body,
        out_shape=jax.ShapeDtypeStruct((2, 64, 24, width), BF),
        grid_spec=pltpu.PrefetchScalarGridSpec(
            num_scalar_prefetch=1,
            grid=(2, 2),
            in_specs=[
                pl.BlockSpec((TOK, 384), lambda i, s, core: (0, ((i + core[0]) % 2) * 2 + s)),
                pl.BlockSpec((TOK, 2 * width), lambda i, s, core: (0, 0)),
                pl.BlockSpec((2, 384, 768), lambda i, s, core: (0, 0, 0)),
            ],
            out_specs=pl.BlockSpec((1, 32, 24, width), lambda i, s, core: (i, s, 0, 0)),
        ),
        compiler_params=pltpu.CompilerParams(vmem_limit_bytes=40 * MIB),
        cost_estimate=pl.CostEstimate(
            flops=4 * TOK * D * 2 * width, bytes_accessed=4 * D * width, transcendentals=0
        ),
        name="owner_grad",
    )(core, left, right, spread)


beta_first = 0.9
beta_second = 0.95
adam_epsilon = 1e-08
gain_rate = 3.0
matrix_decay = 0.1
rope_base = 10000.0
ALL = ("dp", "context", "experts")
OWNERS = ("dp", "experts")
LINE = ("context", "experts")
Y_GROUPS = [[0, 1, 2, 3], [4, 5, 6, 7]]


def send_z(value, hop):
    pairs = [(z * 2 + h, ((z + hop) % 4) * 2 + h) for z in range(4) for h in range(2)]
    return lax.ppermute(value, "context", pairs)


def swap_xh(value):
    pairs = [(z * 2 + h, z * 2 + 1 - h) for z in range(4) for h in range(2)]
    return lax.ppermute(value, "context", pairs)


def send_y(value, hop):
    pairs = [(l * 4 + y, l * 4 + (y + hop) % 4) for l in range(2) for y in range(4)]
    return lax.ppermute(value, "experts", pairs)


def swap_xl(value):
    pairs = [(l * 4 + y, (1 - l) * 4 + y) for l in range(2) for y in range(4)]
    return lax.ppermute(value, "experts", pairs)


def swap_core(value):
    return lax.ppermute(value, "dp", [(0, 1), (1, 0)])


def place():
    context = lax.axis_index("context")
    experts = lax.axis_index("experts")
    return dict(d=lax.axis_index("dp"), z=context // 2, xh=context % 2, xl=experts // 4, y=experts % 4)


def ordered(flag, own, other):
    return jnp.where(flag == 0, jnp.stack([own, other]), jnp.stack([other, own]))


def keep_and_give(pair, flag):
    return (
        lax.dynamic_index_in_dim(pair, flag, 0, False),
        lax.dynamic_index_in_dim(pair, 1 - flag, 0, False),
    )


def rope_tables(positions):
    frequency = rope_base ** (jnp.arange(HD // 2, dtype=F32) * (-2.0 / HD))
    angles = positions.astype(F32)[:, None] * frequency[None, :]
    cosine, sine = jnp.cos(angles), jnp.sin(angles)
    return jnp.concatenate([cosine, cosine], axis=1), jnp.concatenate([-sine, sine], axis=1)


def adam_update(weight, first_moment, second_moment, gradient, step_rate, decay_term):
    first_new = beta_first * first_moment + (1.0 - beta_first) * gradient
    second_new = beta_second * second_moment + (1.0 - beta_second) * gradient * gradient
    first_hat = first_new / (1.0 - beta_first**STEP)
    second_hat = second_new / (1.0 - beta_second**STEP)
    weight_new = weight - step_rate * (
        first_hat / (jnp.sqrt(second_hat) + adam_epsilon) + decay_term * weight
    )
    return (weight_new, first_new, second_new)


def routing(ids, gates):
    flat = ids.reshape(-1)
    one_hot = (flat[:, None] == jnp.arange(EXPERTS, dtype=jnp.int32)).astype(jnp.int32)
    earlier = jnp.cumsum(one_hot, axis=0) - one_hot
    rank = jnp.sum(earlier * one_hot, axis=-1)
    owner = (flat % 2) * (EXPERTS // 2) + flat // 2
    slots = (owner * CAP + rank).reshape(ids.shape)
    hit = slots[:, :, None] == jnp.arange(ROWS, dtype=jnp.int32)
    pick = jnp.any(hit, axis=1).astype(BF)
    weight = jnp.sum(jnp.where(hit, gates[:, :, None], 0.0), axis=1)
    slot_gate = jnp.sum(weight, axis=0)[:, None]
    weight_high, weight_low = split(weight)
    return pick, pick.T, weight_high, weight_low, slot_gate


def exchange(rows):
    return lax.all_to_all(
        rows.reshape(EXPERTS, CAP, D), OWNERS, split_axis=0, concat_axis=0, tiled=True
    ).reshape(ROWS, D)


def gather_keys(rows):
    pair = ordered(place()["xh"], rows, swap_xh(rows))
    return [pair] + [send_z(pair, k) for k in (1, 2, 3)]


def return_keys(grads):
    total = grads[0].astype(F32)
    for k in (1, 2, 3):
        total = total + send_z(grads[k], -k).astype(F32)
    own, other = keep_and_give(total, place()["xh"])
    return own + swap_xh(other.astype(BF)).astype(F32)


def column_blocks(qkv_weight, out_weight):
    return jnp.concatenate(
        [
            qkv_weight.astype(BF).reshape(LAYERS, -1, 4, YQ),
            out_weight.astype(BF).transpose(0, 2, 1).reshape(LAYERS, -1, 4, YO),
        ],
        axis=-1,
    ).transpose(2, 0, 1, 3)


def core_pair(in_weight, down_weight):
    both = jnp.concatenate(
        [in_weight.astype(BF), down_weight.astype(BF).transpose(0, 2, 1)], axis=-1
    )
    own, give = keep_and_give(both, lax.axis_index("dp"))
    return own, swap_core(give)


def scatter_wide(grads):
    at = place()
    width = YQ + YO
    half = (grads[0].astype(F32) + swap_core(grads[1]).astype(F32)).astype(BF)
    total = lax.dynamic_index_in_dim(half, at["y"], 0, False).astype(F32)
    for k in (1, 2, 3):
        chunk = lax.dynamic_index_in_dim(half, (at["y"] + k) % 4, 0, False)
        total = total + send_y(chunk, k).astype(F32)
    part = total.astype(BF).reshape(4, 192, width)
    total = lax.dynamic_index_in_dim(part, at["z"], 0, False).astype(F32)
    for k in (1, 2, 3):
        chunk = lax.dynamic_index_in_dim(part, (at["z"] + k) % 4, 0, False)
        total = total + send_z(chunk, k).astype(F32)
    for flag, swap, rows in ((at["xh"], swap_xh, 96), (at["xl"], swap_xl, 48)):
        kept, other = keep_and_give(total.reshape(2, rows, width), flag)
        total = kept + swap(other.astype(BF)).astype(F32)
    last = lax.all_to_all(
        total.astype(BF).reshape(4, 12, width),
        "experts",
        0,
        0,
        axis_index_groups=Y_GROUPS,
        tiled=True,
    )
    last = last.astype(F32).transpose(1, 0, 2)
    return last[:, :, :YQ].reshape(12, QKV), last[:, :, YQ:].reshape(12, QW)


def scatter_owner(grads):
    half = (grads[0].astype(F32) + swap_core(grads[1]).astype(F32)).astype(BF)
    parts = lax.all_to_all(half, LINE, 0, 0, tiled=True)
    total = jnp.sum(parts.astype(F32), axis=0)
    return jnp.concatenate([total[:12], total[12:]], axis=1)


def scatter_experts(grads):
    pair = lax.psum_scatter(grads, "context", scatter_dimension=0)
    core = lax.axis_index("dp")
    own, give = keep_and_give(pair, core)
    return ordered(core, own, swap_core(give)).astype(F32)


def spread_gains(rows):
    return rows.reshape(4, 128, 12).transpose(1, 0, 2).reshape(128, 1, 48)


def local(
    tokens,
    cotangent,
    expert_ids,
    gate_values,
    block_order,
    qkv_weight,
    qkv_first,
    qkv_second,
    out_weight,
    out_first,
    out_second,
    in_weight,
    in_first,
    in_second,
    down_weight,
    down_first,
    down_second,
    norm_gains,
    gain_first,
    gain_second,
):
    at = place()
    core = at["d"].astype(jnp.int32).reshape(1)
    blocks = lax.all_to_all(
        column_blocks(qkv_weight, out_weight),
        "experts",
        0,
        0,
        axis_index_groups=Y_GROUPS,
        tiled=True,
    ).transpose(1, 0, 2, 3)
    projections = [
        lax.all_gather(blocks[l].reshape(48, YQ + YO), ALL, axis=0).reshape(32, 4, 48, YQ + YO)
        for l in range(LAYERS)
    ]
    gain_rows = norm_gains.astype(BF).astype(F32).reshape(1, 1, 48)
    gains = lax.all_to_all(jnp.broadcast_to(gain_rows, (128, 1, 48)), ALL, 0, 0, tiled=True)
    gains = gains.reshape(128, 4, 12).transpose(1, 0, 2).reshape(4, 1, D)

    own, other = core_pair(in_weight[0], down_weight[0])
    column = [own] + [send_z(own, k) for k in (1, 2, 3)]
    beside = [swap_xh(rows) for rows in column]
    pair = ordered(at["xh"], other, swap_xh(other))
    pairs = [pair] + [send_z(pair, k) for k in (1, 2, 3)]
    turns = (at["z"] - jnp.arange(4, dtype=jnp.int32)) % 4
    both = jnp.arange(2, dtype=jnp.int32)
    direct_places = jnp.concatenate(
        [
            at["d"] * 8 + turns * 2 + at["xh"],
            at["d"] * 8 + turns * 2 + 1 - at["xh"],
            ((1 - at["d"]) * 8 + turns[:, None] * 2 + both[None, :]).reshape(-1),
        ]
    ).astype(jnp.int32)
    gathered_places = (
        jnp.arange(8, dtype=jnp.int32)[:, None] + 8 * both[None, :]
    ).reshape(-1)
    later = ordered(at["d"], *core_pair(in_weight[1], down_weight[1]))
    experts = [
        (column + beside + pairs, direct_places),
        ([lax.all_gather(later, "context", axis=0)], gathered_places),
    ]

    order_row = block_order[0]
    offsets = jnp.arange(TOK, dtype=jnp.int32)
    places = jnp.arange(8, dtype=jnp.int32)
    source = (turns[:, None] * 2 + both[None, :]).reshape(-1)
    key_block = jnp.sum(jnp.where(source[:, None] == places, order_row, 0), axis=1)
    own_block = jnp.sum(jnp.where(places == lax.axis_index("context"), order_row, 0))
    query_pos = own_block * TOK + offsets
    key_pos = (key_block[:, None] * TOK + offsets[None, :]).reshape(-1, 1)
    cosine, sine = rope_tables(query_pos)
    query_pos = query_pos.reshape(1, -1)
    routes = [routing(expert_ids[l, 0], gate_values[l, 0]) for l in range(LAYERS)]
    spread = spread_matrices()

    saved = []
    base, came_back = tokens[0], None
    for l in range(LAYERS):
        pick, pick_t, weight_high, weight_low, slot_gate = routes[l]
        if l == 0:
            attn_in, scale_one, qkv = project(base, gains[0], cosine, sine, projections[0])
        else:
            base, attn_in, scale_one, qkv = project(
                base, gains[2 * l], cosine, sine, projections[l], came_back
            )
        kv = gather_keys(qkv[:, QW:])
        mixed, level = attend(qkv, kv, key_pos, query_pos)
        middle, scale_two, sent = branch(base, mixed, gains[2 * l + 1], pick_t, projections[l])
        received = exchange(sent)
        weights, chunk_places = experts[l]
        returned, hidden, act, slope = ffn(received, weights, chunk_places)
        came_back = (exchange(returned), weight_high, weight_low)
        saved.append(
            (base, attn_in, scale_one, qkv, kv, mixed, level, middle, scale_two, received, hidden, act, slope)
        )
        base = middle
    result = middle + (
        dot(came_back[1], came_back[0], NN) + dot(came_back[2], came_back[0], NN)
    )

    d_out = cotangent[0]
    pick_t, slot_gate = routes[-1][1], routes[-1][4]
    sent = (dot(pick_t, d_out, NN) * slot_gate).astype(BF)
    projection_sums = [None] * LAYERS
    expert_sums = [None] * LAYERS
    gain_grads = [None] * (2 * LAYERS)
    for l in reversed(range(LAYERS)):
        (base, attn_in, scale_one, qkv, kv, mixed, level, middle, scale_two, received, hidden, act, slope) = (
            saved[l]
        )
        weights, chunk_places = experts[l]
        owner = exchange(sent)
        d_rows, d_both = ffn_back(owner, act, slope, weights, chunk_places)
        came_grad = exchange(d_rows)
        expert_grad = ffn_grad(received, d_both, owner, hidden)
        if l < LAYERS - 1:
            expert_grad, expert_sums[l + 1] = lax.optimization_barrier(
                (expert_grad, expert_sums[l + 1])
            )
        expert_sums[l] = scatter_experts(expert_grad)
        d_base, d_branch, d_mixed, gain_grads[2 * l + 1] = branch_back(
            came_grad, routes[l][0], middle, scale_two, gains[2 * l + 1], d_out, projections[l]
        )
        if l == 0:
            out_rows = scatter_owner(owner_grad(core, d_branch, mixed, spread))
        d_queries, d_pairs = attend_back(qkv, kv, key_pos, query_pos, level, d_mixed)
        d_key_value = return_keys(d_pairs.reshape(4, 2, TOK, 2 * KW))
        extra = (routes[l - 1][1], routes[l - 1][4]) if l else None
        back = project_back(
            d_queries,
            d_key_value,
            cosine,
            sine,
            base,
            scale_one,
            gains[2 * l],
            d_base,
            projections[l],
            extra,
        )
        d_out, d_projected, gain_grads[2 * l] = back[:3]
        if l:
            sent = back[3]
            projection_sums[l] = scatter_wide(
                wide_grad(core, attn_in, d_projected, d_branch, mixed)
            )
        else:
            projection_sums[l] = (
                scatter_owner(owner_grad(core, attn_in, d_projected, spread)),
                out_rows,
            )
    gain_sum = lax.all_to_all(
        spread_gains(jnp.concatenate(gain_grads, axis=0)), ALL, 0, 0, tiled=True
    )
    gain_sum = jnp.sum(gain_sum, axis=0).reshape(2, 2, 12)
    qkv_sum = jnp.stack([s[0] for s in projection_sums])
    out_sum = jnp.stack([s[1] for s in projection_sums]).transpose(0, 2, 1)
    in_sum = jnp.stack([s[:, :, : 2 * FF] for s in expert_sums])
    down_sum = jnp.stack([s[:, :, 2 * FF :] for s in expert_sums]).transpose(0, 1, 3, 2)
    wide_rate = 5.0 * D ** (-0.5)
    out_rate = 5.0 * (HQ * HD / 16.0) ** (-0.5)
    down_rate = 5.0 * (FF / 4.0) ** (-0.5)
    updates = (
        adam_update(qkv_weight, qkv_first, qkv_second, qkv_sum, wide_rate, matrix_decay)
        + adam_update(out_weight, out_first, out_second, out_sum, out_rate, matrix_decay)
        + adam_update(in_weight, in_first, in_second, in_sum, wide_rate, matrix_decay)
        + adam_update(down_weight, down_first, down_second, down_sum, down_rate, matrix_decay)
        + adam_update(norm_gains, gain_first, gain_second, gain_sum, gain_rate, 0.0)
    )
    return (result.astype(BF)[None], d_out[None]) + updates


def solution(mesh):
    rows = P(("dp", "experts"), "context", None)
    routes = P(None, ("dp", "experts"), "context", None)
    qkv = P(None, ALL, None)
    out = P(None, None, ALL)
    wide = P(None, "experts", ("dp", "context"), None)
    down = P(None, "experts", None, ("dp", "context"))
    states = (qkv,) * 3 + (out,) * 3 + (wide,) * 3 + (down,) * 3 + (out,) * 3
    return jax.shard_map(
        local,
        mesh=mesh,
        in_specs=(rows, rows, routes, routes, P(("dp", "experts"), None)) + states,
        out_specs=(rows, rows) + states,
        check_vma=False,
    )
```

time: 2390 us -> 901 us (0.38)
  blocking collectives: 867 us -> 50.5 us
  waiting for transfers between devices: 818 us -> 400 us
  local copies, waits for them, and re-layouts: 350 us -> 105 us
  matrix products: 158 us -> 7.75 us
  Pallas kernels: 0 us -> 136 us
  starting transfers between devices: 31 us -> 119 us
  other arithmetic: 134 us -> 55.8 us
    unnamed x19 -> x5, waiting for transfers between devices: 644 us -> 0.1 us
    all_gather x5 -> x0, blocking collectives: 490 us -> none  [the longest x1 376 us: local(): lax.all_gather(low_gain, ('dp', 'context', 'experts'), axis=2, tiled=True)]
    unnamed x1 -> x0, blocking collectives: 325 us -> none
    ppermute x0 -> x42, waiting for transfers between devices: none -> 198 us  [the longest x10 83.6 us: swap_xh(): return lax.ppermute(value, 'context', pairs)]
    reduce_scatter x1 -> x2, waiting for transfers between devices: 159 us -> 7.65 us  [scatter_experts(): pair = lax.psum_scatter(grads, 'context', scatter_dimension=0)]
    dot_general x34 -> x3, matrix products: 149 us -> 7.75 us  [dot(): lax.dot_general(a, b, (contract, ((), ())), preferred_element_type=F32)]
    pallas_call x0 -> x21, Pallas kernels: none -> 136 us  [the longest x18 124 us: call(): pl.pallas_call(body, out_shape=[jax.ShapeDtypeStruct(s, t) for s, t in ou...]
    all_to_all x6 -> x12, waiting for transfers between devices: 14.8 us -> 144 us  [the longest x7 88.7 us: exchange(): lax.all_to_all(rows.reshape(EXPERTS, CAP, D), OWNERS, split_axis=0, conca...]
  transfers between devices with their start and end apart: 18 -> 59, of which waited for: 8 -> 36; matrix products, arithmetic and copies ran while one was open for 20% -> 10% of each run, Pallas kernels for 0% -> 13%
where the time goes in v1:
time: 901 us; the launch traced here: 891 us
  waiting for transfers between devices  400 us (44%)
  Pallas kernels  136 us (15%)
  starting transfers between devices  119 us (13%)
  local copies, waits for them, and re-layouts  105 us (12%)
  other arithmetic  55.8 us (6%)
  blocking collectives  50.5 us (6%)
  between operations  16.9 us (2%)
    pallas_call x18, Pallas kernels, call(): pl.pallas_call(body, out_shape=[jax.ShapeDtypeStruct(s, t) for s, t in ou...  124 us
    all_to_all x7, waiting for transfers between devices, exchange(): lax.all_to_all(rows.reshape(EXPERTS, CAP, D), OWNERS, split_axis=0, conca...  88.7 us
    ppermute x10, waiting for transfers between devices, swap_xh(): return lax.ppermute(value, 'context', pairs)  83.6 us
    unnamed x304, local copies, waits for them, and re-layouts  74.4 us
    ppermute x21, waiting for transfers between devices, send_z(): return lax.ppermute(value, 'context', pairs)  65.7 us
    all_gather x2, waiting for transfers between devices, local(): lax.all_gather(blocks[l].reshape(48, YQ + YO), ALL, axis=0)  49.3 us
    ppermute x3, waiting for transfers between devices, send_y(): return lax.ppermute(value, 'experts', pairs)  47.5 us
    all_to_all x2, waiting for transfers between devices, scatter_owner(): parts = lax.all_to_all(half, LINE, 0, 0, tiled=True)  46.5 us
  transfers between devices with their start and end apart: 59, of which 36 were waited for; matrix products, arithmetic and copies ran while one was open for 10% of the time, Pallas kernels for 13%

profile of v1, /device:TPU:1, one launch (start us, length us, event | category | flops | bytes accessed | tf_op | source)
XLA Modules:
  0.0 890.9 jit_solution(4530662368602738482)
XLA Ops:
  9.7 9.9 %all_to_all.70 = bf16[4,2,12,896]{3,1,2,0:T(2,128)(2,1)S(1)} all-to-all(bf16[4,2,12,896]{3,1,2,0:T(2,128)(2,1)S(1)} %copy.227), channel_id=1, replica_groups={{0,1,2,3},{4,5,6,7},{8,9,10,11},{12,13,14,15},{16,17,18,19},{20,21,22,2..., dimensions={0} | all-to-all | bytes 344064 | tf_op jit(solution)/shard_map/all_to_all | solution.py:730
  46.3 49.3 %all-gather.4.cloned.1.call-done = bf16[128,48,896]{2,1,0:T(8,128)(2,1)} async-done(((bf16[1,48,896]{2,1,0:T(8,128)(2,1)}), bf16[128,48,896]{2,1,0:T(8,128)(2,1)}) %all-gather.4.cloned.1.call-update) | async-done | bytes 11010064 | tf_op jit(solution)/shard_map/all_gather | solution.py:739
  152.1 10.2 %collective-permute-done.4.refs_1_ = bf16[96,2304]{1,0:T(8,128)(2,1)} collective-permute-done((bf16[96,2304]{1,0:T(8,128)(2,1)}, bf16[96,2304]{1,0:T(8,128)(2,1)}, u32[]{:S(2)}, u32[]{:S(2)}) %collective-permute-start.4) | collective-permute-done | bytes 442400 | tf_op jit(solution)/shard_map/ppermute | solution.py:551
  164.5 29.8 %collective-permute-done.12 = bf16[96,2304]{1,0:T(8,128)(2,1)S(1)} collective-permute-done((bf16[96,2304]{1,0:T(8,128)(2,1)}, bf16[96,2304]{1,0:T(8,128)(2,1)S(1)}, u32[]{:S(2)}, u32[]{:S(2)}) %collective-permute-start.12) | collective-permute-done | bytes 442400 | tf_op jit(solution)/shard_map/ppermute | solution.py:556
  204.4 8.9 %collective-permute-done.8.refs_5_ = bf16[96,2304]{1,0:T(8,128)(2,1)} collective-permute-done((bf16[96,2304]{1,0:T(8,128)(2,1)}, bf16[96,2304]{1,0:T(8,128)(2,1)}, u32[]{:S(2)}, u32[]{:S(2)}) %collective-permute-start.8) | collective-permute-done | bytes 442400 | tf_op jit(solution)/shard_map/ppermute | solution.py:556
  214.2 8.7 collective-permute-done.9.refs_6_
  222.8 9.5 %collective-permute-done.10.refs_7_ = bf16[96,2304]{1,0:T(8,128)(2,1)} collective-permute-done((bf16[96,2304]{1,0:T(8,128)(2,1)}, bf16[96,2304]{1,0:T(8,128)(2,1)}, u32[]{:S(2)}, u32[]{:S(2)}) %collective-permute-start.10) | collective-permute-done | bytes 442400 | tf_op jit(solution)/shard_map/ppermute | solution.py:556
  240.6 9.5 %ffn.2 = (bf16[640,1536]{1,0:T(8,128)(2,1)S(1)}, bf16[640,768]{1,0:T(8,128)(2,1)S(1)}, f32[640,768]{1,0:T(8,128)S(1)}, f32[640,768]{1,0:T(8,128)S(1)}) custom-call(s32[16]{0:T(128)S(1)} %pad_add_fusion.places, bf16[640,1536]{1,0:T(8,128)(2,1)} %bitcast.286, bf16[96,2304]{1,0:T(8,128)(2,1)S(1)} %copy-done.42, ...), custom_call_target="tpu_custom_call" | custom-call | flops 4529848320 | bytes 14942208 | tf_op jit(solution)/shard_map/ffn/pallas_call | solution.py:64
  263.0 31.8 %all-to-all-done.3 = bf16[16,40,1536]{2,1,0:T(8,128)(2,1)S(1)} async-done(((bf16[16,40,1536]{2,1,0:T(8,128)(2,1)}), bf16[16,40,1536]{2,1,0:T(8,128)(2,1)S(1)}, u32[]{:S(2)}, u32[]{:S(2)}) %all-to-all-start.3) | async-done | bytes 1966112 | tf_op jit(solution)/shard_map/all_to_all | solution.py:624
  301.4 8.8 collective-permute-done.16
  358.2 21.7 %all-to-all-done.4 = bf16[16,40,1536]{2,1,0:T(8,128)(2,1)} async-done(((bf16[16,40,1536]{2,1,0:T(8,128)(2,1)}), bf16[16,40,1536]{2,1,0:T(8,128)(2,1)}, u32[]{:S(2)}, u32[]{:S(2)}) %all-to-all-start.4) | async-done | bytes 1966112 | tf_op jit(solution)/shard_map/all_to_all | solution.py:624
  384.6 9.4 %ffn.3 = (bf16[640,1536]{1,0:T(8,128)(2,1)S(1)}, bf16[640,768]{1,0:T(8,128)(2,1)S(1)}, f32[640,768]{1,0:T(8,128)S(1)}, f32[640,768]{1,0:T(8,128)S(1)}) custom-call(s32[16]{0:T(128)S(1)} %add.544.places, bf16[640,1536]{1,0:T(8,128)(2,1)} %bitcast.33.received, bf16[8,2,96,2304]{3,2,1,0:T(8,128)(2,1)} %all-gather.8.cloned.1.call-done.refs_0_), custom_call_target="tpu_custom_call" | custom-call | flops 4529848320 | bytes 14942208 | tf_op jit(solution)/shard_map/ffn/pallas_call | solution.py:64
  398.8 11.9 %all-to-all-done.6 = bf16[16,40,1536]{2,1,0:T(8,128)(2,1)} async-done(((bf16[16,40,1536]{2,1,0:T(8,128)(2,1)}), bf16[16,40,1536]{2,1,0:T(8,128)(2,1)}, u32[]{:S(2)}, u32[]{:S(2)}) %all-to-all-start.6) | async-done | bytes 1966112 | tf_op jit(solution)/shard_map/all_to_all | solution.py:624
  413.8 9.5 %ffn_back.2 = (bf16[640,1536]{1,0:T(8,128)(2,1)S(1)}, bf16[640,1536]{1,0:T(8,128)(2,1)S(1)}) custom-call(s32[16]{0:T(128)S(1)} %add.544.places, bf16[640,1536]{1,0:T(8,128)(2,1)} %bitcast.45.owner, f32[640,768]{1,0:T(8,128)S(1)} %copy-done.95, f32[640,768]{1,0:T(8,128)S(1)} %copy-done.97, bf16[8,2,96,2304]{3,2,1,0:T(8,128)(2,1)} %all-gather.8.cloned.1.call-done.refs_0_), custom_call_target="tpu_custom_call" | custom-call | flops 4529848320 | bytes 14942208 | tf_op jit(solution)/shard_map/ffn_back/pallas_call | solution.py:64
  435.4 40.6 %all_to_all.71 = bf16[16,40,1536]{2,1,0:T(8,128)(2,1)S(1)} all-to-all(bf16[16,40,1536]{2,1,0:T(8,128)(2,1)} %bitcast.294), channel_id=1, replica_groups=mesh['dp'=2,'context'=8,'experts'=8] {'dp','experts'}, dimensions={0} | all-to-all | bytes 3932160 | tf_op jit(solution)/shard_map/all_to_all | solution.py:624
  480.9 11.0 %attend_back.2 = (f32[128,1536]{1,0:T(8,128)S(1)}, bf16[1024,512]{1,0:T(8,128)(2,1)S(1)}) custom-call(bf16[128,2048]{1,0:T(8,128)(2,1)S(1)} %copy-done.66, bf16[2,128,512]{2,1,0:T(8,128)(2,1)S(1)} %copy-done.55, bf16[2,128,512]{2,1,0:T(8,128)(2,1)S(1)} %copy-done.81, bf16[2,128,512]{2,1,0:T(8,128)(2,1)S(1)} %copy-done.84, ...), custom_call_target="tpu_custom_call" | custom-call | flops 2013265920 | bytes 2097152 | tf_op jit(solution)/shard_map/attend_back/pallas_call | solution.py:64
  556.4 14.9 %all-to-all-done.8 = bf16[16,40,1536]{2,1,0:T(8,128)(2,1)S(1)} async-done(((bf16[16,40,1536]{2,1,0:T(8,128)(2,1)}), bf16[16,40,1536]{2,1,0:T(8,128)(2,1)S(1)}, u32[]{:S(2)}, u32[]{:S(2)}) %all-to-all-start.8) | async-done | bytes 1966112 | tf_op jit(solution)/shard_map/all_to_all | solution.py:624
  571.3 10.6 %ffn_back.3 = (bf16[640,1536]{1,0:T(8,128)(2,1)S(1)}, bf16[640,1536]{1,0:T(8,128)(2,1)S(1)}) custom-call(s32[16]{0:T(128)S(1)} %pad_add_fusion.places, bf16[640,1536]{1,0:T(8,128)(2,1)S(1)} %bitcast.290, f32[640,768]{1,0:T(8,128)} %copy-done.92, f32[640,768]{1,0:T(8,128)} %copy-done.93, bf16[96,2304]{1,0:T(8,128)(2,1)S(1)} %copy-done.43, ...), custom_call_target="tpu_custom_call" | custom-call | flops 4529848320 | bytes 14942208 | tf_op jit(solution)/shard_map/ffn_back/pallas_call | solution.py:64
  626.6 11.0 %attend_back.3 = (f32[128,1536]{1,0:T(8,128)S(1)}, bf16[1024,512]{1,0:T(8,128)(2,1)S(1)}) custom-call(bf16[128,2048]{1,0:T(8,128)(2,1)S(1)} %copy-done.63, bf16[2,128,512]{2,1,0:T(8,128)(2,1)S(1)} %copy-done.53, bf16[2,128,512]{2,1,0:T(8,128)(2,1)S(1)} %copy-done.74, bf16[2,128,512]{2,1,0:T(8,128)(2,1)S(1)} %copy-done.76, ...), custom_call_target="tpu_custom_call" | custom-call | flops 2013265920 | bytes 2097152 | tf_op jit(solution)/shard_map/attend_back/pallas_call | solution.py:64
  676.9 12.2 %collective-permute-done.33 = bf16[768,896]{1,0:T(8,128)(2,1)} collective-permute-done((bf16[768,896]{1,0:T(8,128)(2,1)}, bf16[768,896]{1,0:T(8,128)(2,1)}, u32[]{:S(2)}, u32[]{:S(2)}) %collective-permute-start.33) | collective-permute-done | bytes 1376288 | tf_op jit(solution)/shard_map/ppermute | solution.py:561
  692.1 32.3 %collective-permute-done.31 = bf16[768,896]{1,0:T(8,128)(2,1)} collective-permute-done((bf16[768,896]{1,0:T(8,128)(2,1)}, bf16[768,896]{1,0:T(8,128)(2,1)}, u32[]{:S(2)}, u32[]{:S(2)}) %collective-permute-start.31) | collective-permute-done | bytes 1376288 | tf_op jit(solution)/shard_map/ppermute | solution.py:561
  763.8 8.8 all-to-all-done.13
  794.1 24.4 %all-to-all-done.12 = bf16[64,24,768]{2,1,0:T(8,128)(2,1)S(1)} async-done(((bf16[64,24,768]{2,1,0:T(8,128)(2,1)}), bf16[64,24,768]{2,1,0:T(8,128)(2,1)S(1)}, u32[]{:S(2)}, u32[]{:S(2)}) %all-to-all-start.12) | async-done | bytes 2359328 | tf_op jit(solution)/shard_map/all_to_all | solution.py:690
  841.5 22.1 %all-to-all-done.10 = bf16[64,24,1024]{2,1,0:T(8,128)(2,1)S(1)} async-done(((bf16[64,24,1024]{2,1,0:T(8,128)(2,1)}), bf16[64,24,1024]{2,1,0:T(8,128)(2,1)S(1)}, u32[]{:S(2)}, u32[]{:S(2)}) %all-to-all-start.10) | async-done | bytes 3145760 | tf_op jit(solution)/shard_map/all_to_all | solution.py:690
  (581 shorter events, 457.2 us)
Async XLA Ops:
  7.2 88.4 %all-gather.4.cloned.1.call-start = ((), (), s32[]{:S(2)}) async-start(), calls=%async_computation.16 | async-start | bytes 11096064 | tf_op jit(solution)/shard_map/all_gather | solution.py:739
  21.0 242.0 %all-gather.6.cloned.1.call-start = ((), (), s32[]{:S(2)}) async-start(), calls=%async_computation.17 | async-start | bytes 11096064 | tf_op jit(solution)/shard_map/all_gather | solution.py:739
  34.9 349.7 %all-gather.8.cloned.1.call-start = ((), (), s32[]{:S(2)}) async-start(), calls=%async_computation.18 | async-start | bytes 7962624 | tf_op jit(solution)/shard_map/all_gather | solution.py:766
  35.9 110.5 %collective-permute-start.11 = (bf16[96,2304]{1,0:T(8,128)(2,1)}, bf16[96,2304]{1,0:T(8,128)(2,1)}, u32[]{:S(2)}, u32[]{:S(2)}) collective-permute-start(bf16[96,2304]{1,0:T(8,128)(2,1)} %get-tuple-element.264), channel_id=1, source_target_pairs={{0,64},{64,0},{1,65},{65,1},{2,66},{66,2},{3,67},{67,3},{4,68},{68... | collective-permute-start | bytes 1327112 | tf_op jit(solution)/shard_map/ppermute | solution.py:570
  139.8 98.5 %all-to-all-start.2 = ((bf16[16,40,1536]{2,1,0:T(8,128)(2,1)}), bf16[16,40,1536]{2,1,0:T(8,128)(2,1)S(1)}, u32[]{:S(2)}, u32[]{:S(2)}) async-start(bf16[16,40,1536]{2,1,0:T(8,128)(2,1)} %bitcast.289), calls=%async_computation.2 | async-start | bytes 3932160 | tf_op jit(solution)/shard_map/all_to_all | solution.py:624
  146.4 47.9 %collective-permute-start.12 = (bf16[96,2304]{1,0:T(8,128)(2,1)}, bf16[96,2304]{1,0:T(8,128)(2,1)S(1)}, u32[]{:S(2)}, u32[]{:S(2)}) collective-permute-start(bf16[96,2304]{1,0:T(8,128)(2,1)} %collective-permute-done.11), channel_id=1, source_target_pairs={{0,8},{8,0},{16,24},{24,16},{32,40},{40,32},{48,56},{56,48},{1,9},... | collective-permute-start | bytes 1327112 | tf_op jit(solution)/shard_map/ppermute | solution.py:556
  148.6 48.7 %collective-permute-start.5 = (bf16[96,2304]{1,0:T(8,128)(2,1)}, bf16[96,2304]{1,0:T(8,128)(2,1)}, u32[]{:S(2)}, u32[]{:S(2)}) collective-permute-start(bf16[96,2304]{1,0:T(8,128)(2,1)} %get-tuple-element.265.refs_0_), channel_id=1, source_target_pairs={{0,32},{8,40},{16,48},{24,56},{32,0},{40,8},{48,16},{56,24},{1,33}... | collective-permute-start | bytes 1327112 | tf_op jit(solution)/shard_map/ppermute | solution.py:551
  151.5 48.7 %collective-permute-start.6 = (bf16[96,2304]{1,0:T(8,128)(2,1)}, bf16[96,2304]{1,0:T(8,128)(2,1)}, u32[]{:S(2)}, u32[]{:S(2)}) collective-permute-start(bf16[96,2304]{1,0:T(8,128)(2,1)} %get-tuple-element.265.refs_0_), channel_id=1, source_target_pairs={{0,48},{8,56},{16,0},{24,8},{32,16},{40,24},{48,32},{56,40},{1,49}... | collective-permute-start | bytes 1327112 | tf_op jit(solution)/shard_map/ppermute | solution.py:551
  151.5 52.4 %collective-permute-start.7 = (bf16[96,2304]{1,0:T(8,128)(2,1)}, bf16[96,2304]{1,0:T(8,128)(2,1)}, u32[]{:S(2)}, u32[]{:S(2)}) collective-permute-start(bf16[96,2304]{1,0:T(8,128)(2,1)} %get-tuple-element.265.refs_0_), channel_id=1, source_target_pairs={{0,8},{8,0},{16,24},{24,16},{32,40},{40,32},{48,56},{56,48},{1,9},... | collective-permute-start | bytes 1327112 | tf_op jit(solution)/shard_map/ppermute | solution.py:556
  162.3 51.0 %collective-permute-start.8 = (bf16[96,2304]{1,0:T(8,128)(2,1)}, bf16[96,2304]{1,0:T(8,128)(2,1)}, u32[]{:S(2)}, u32[]{:S(2)}) collective-permute-start(bf16[96,2304]{1,0:T(8,128)(2,1)} %collective-permute-done.4.refs_1_), channel_id=1, source_target_pairs={{0,8},{8,0},{16,24},{24,16},{32,40},{40,32},{48,56},{56,48},{1,9},... | collective-permute-start | bytes 1327112 | tf_op jit(solution)/shard_map/ppermute | solution.py:556
  197.3 41.0 %collective-permute-start.14 = (bf16[2,96,2304]{2,1,0:T(8,128)(2,1)}, bf16[2,96,2304]{2,1,0:T(8,128)(2,1)}, u32[]{:S(2)}, u32[]{:S(2)}) collective-permute-start(bf16[2,96,2304]{2,1,0:T(8,128)(2,1)} %maximum_select_fusion.refs_8_), channel_id=1, source_target_pairs={{0,32},{8,40},{16,48},{24,56},{32,0},{40,8},{48,16},{56,24},{1,33}... | collective-permute-start | bytes 2654216 | tf_op jit(solution)/shard_map/ppermute | solution.py:551
  200.2 38.2 %collective-permute-start.15 = (bf16[2,96,2304]{2,1,0:T(8,128)(2,1)}, bf16[2,96,2304]{2,1,0:T(8,128)(2,1)}, u32[]{:S(2)}, u32[]{:S(2)}) collective-permute-start(bf16[2,96,2304]{2,1,0:T(8,128)(2,1)} %maximum_select_fusion.refs_8_), channel_id=1, source_target_pairs={{0,48},{8,56},{16,0},{24,8},{32,16},{40,24},{48,32},{56,40},{1,49}... | collective-permute-start | bytes 2654216 | tf_op jit(solution)/shard_map/ppermute | solution.py:551
  255.0 39.9 %all-to-all-start.3 = ((bf16[16,40,1536]{2,1,0:T(8,128)(2,1)}), bf16[16,40,1536]{2,1,0:T(8,128)(2,1)S(1)}, u32[]{:S(2)}, u32[]{:S(2)}) async-start(bf16[16,40,1536]{2,1,0:T(8,128)(2,1)} %bitcast.293), calls=%async_computation.3 | async-start | bytes 3932160 | tf_op jit(solution)/shard_map/all_to_all | solution.py:624
  384.4 168.4 %reduce-scatter.3.cloned.1.call-start = ((), (), s32[]{:S(2)}) async-start(), calls=%async_computation.19 | async-start | bytes 7962624 | tf_op jit(solution)/shard_map/reduce_scatter | solution.py:696
  540.5 98.0 %collective-permute-start.30 = (bf16[4,768,896]{2,1,0:T(8,128)(2,1)}, bf16[4,768,896]{2,1,0:T(8,128)(2,1)}, u32[]{:S(2)}, u32[]{:S(2)}) collective-permute-start(bf16[4,768,896]{2,1,0:T(8,128)(2,1)} %slice_bitcast_fusion), channel_id=1, source_target_pairs={{0,64},{64,0},{1,65},{65,1},{2,66},{66,2},{3,67},{67,3},{4,68},{68... | collective-permute-start | bytes 16515080 | tf_op jit(solution)/shard_map/ppermute | solution.py:570
  555.0 48.1 %collective-permute-start.40 = (bf16[96,2304]{1,0:T(8,128)(2,1)}, bf16[96,2304]{1,0:T(8,128)(2,1)}, u32[]{:S(2)}, u32[]{:S(2)}) collective-permute-start(bf16[96,2304]{1,0:T(8,128)(2,1)} %get-tuple-element.261), channel_id=1, source_target_pairs={{0,64},{64,0},{1,65},{65,1},{2,66},{66,2},{3,67},{67,3},{4,68},{68... | collective-permute-start | bytes 1327112 | tf_op jit(solution)/shard_map/ppermute | solution.py:570
  589.2 278.4 %reduce-scatter.5.cloned.1.call-start = ((), (), s32[]{:S(2)}) async-start(), calls=%async_computation.20 | async-start | bytes 7962624 | tf_op jit(solution)/shard_map/reduce_scatter | solution.py:696
  649.3 39.8 %collective-permute-start.33 = (bf16[768,896]{1,0:T(8,128)(2,1)}, bf16[768,896]{1,0:T(8,128)(2,1)}, u32[]{:S(2)}, u32[]{:S(2)}) collective-permute-start(bf16[768,896]{1,0:T(8,128)(2,1)} %get-tuple-element.243), channel_id=1, source_target_pairs={{0,3},{1,0},{2,1},{3,2},{4,7},{5,4},{6,5},{7,6},{8,11},{9,8},{10,9... | collective-permute-start | bytes 4128776 | tf_op jit(solution)/shard_map/ppermute | solution.py:561
  650.5 41.6 %collective-permute-start.32 = (bf16[768,896]{1,0:T(8,128)(2,1)}, bf16[768,896]{1,0:T(8,128)(2,1)}, u32[]{:S(2)}, u32[]{:S(2)}) collective-permute-start(bf16[768,896]{1,0:T(8,128)(2,1)} %get-tuple-element.244), channel_id=1, source_target_pairs={{0,2},{1,3},{2,0},{3,1},{4,6},{5,7},{6,4},{7,5},{8,10},{9,11},{10,... | collective-permute-start | bytes 4128776 | tf_op jit(solution)/shard_map/ppermute | solution.py:561
  651.5 72.9 %collective-permute-start.31 = (bf16[768,896]{1,0:T(8,128)(2,1)}, bf16[768,896]{1,0:T(8,128)(2,1)}, u32[]{:S(2)}, u32[]{:S(2)}) collective-permute-start(bf16[768,896]{1,0:T(8,128)(2,1)} %get-tuple-element.242), channel_id=1, source_target_pairs={{0,1},{1,2},{2,3},{3,0},{4,5},{5,6},{6,7},{7,4},{8,9},{9,10},{10,1... | collective-permute-start | bytes 4128776 | tf_op jit(solution)/shard_map/ppermute | solution.py:561
  653.1 104.5 %all-to-all-start.5 = ((bf16[16,40,1536]{2,1,0:T(8,128)(2,1)}), bf16[16,40,1536]{2,1,0:T(8,128)(2,1)}, u32[]{:S(2)}, u32[]{:S(2)}) async-start(bf16[16,40,1536]{2,1,0:T(8,128)(2,1)} %bitcast.285), calls=%async_computation.5 | async-start | bytes 3932160 | tf_op jit(solution)/shard_map/all_to_all | solution.py:624
  670.4 105.5 %collective-permute-start.39 = (bf16[64,24,768]{2,1,0:T(8,128)(2,1)}, bf16[64,24,768]{2,1,0:T(8,128)(2,1)}, u32[]{:S(2)}, u32[]{:S(2)}) collective-permute-start(bf16[64,24,768]{2,1,0:T(8,128)(2,1)} %slice_bitcast_fusion.4), channel_id=1, source_target_pairs={{0,64},{64,0},{1,65},{65,1},{2,66},{66,2},{3,67},{67,3},{4,68},{68... | collective-permute-start | bytes 7077896 | tf_op jit(solution)/shard_map/ppermute | solution.py:570
  675.5 55.3 %collective-permute-start.28 = (bf16[128,512]{1,0:T(8,128)(2,1)S(1)}, bf16[128,512]{1,0:T(8,128)(2,1)S(1)}, u32[]{:S(2)}, u32[]{:S(2)}) collective-permute-start(bf16[128,512]{1,0:T(8,128)(2,1)S(1)} %fusion.42), channel_id=1, source_target_pairs={{0,8},{8,0},{16,24},{24,16},{32,40},{40,32},{48,56},{56,48},{1,9},... | collective-permute-start | bytes 393224 | tf_op jit(solution)/shard_map/ppermute | solution.py:556
  820.0 43.5 %all-to-all-start.10 = ((bf16[64,24,1024]{2,1,0:T(8,128)(2,1)}), bf16[64,24,1024]{2,1,0:T(8,128)(2,1)S(1)}, u32[]{:S(2)}, u32[]{:S(2)}) async-start(bf16[64,24,1024]{2,1,0:T(8,128)(2,1)} %fusion.1), calls=%async_computation.10 | async-start | bytes 6291456 | tf_op jit(solution)/shard_map/all_to_all | solution.py:690
  (184 other events, 2389.3 us)
Sparse Core Ops, SparseCore 0:
  21.2 74.3 all-gather.3
  99.2 89.1 all-gather.5
  191.2 148.2 all-gather.7
  435.5 117.3 reduce-scatter.2
  605.9 115.8 reduce-scatter.4
